TPU v7x, 32 devices: a whole 2x2x4 slice. The times are simulated.
32 devices in a mesh: section: 4 (over z), dp: 8 (over y, x, core).
Axes of the slice: x: 2, y: 2, z: 4, core: 2. Of those that a mesh axis runs over, the one named last changes fastest.
Arguments:
- tokens: int32 [32, 640], P('dp'), may hold values from 0 to 255
- padding_mask: int32 [32, 640], P('dp'), may hold values from 0 to 1, as said below
- embedding: float32 [512, 256], P('dp', 'section'), may hold values from -0.5 to 0.5
- mixer_weight: float32 [2, 512, 1536], P(None, 'dp'), may hold values from -0.25 to 0.25
- output_weight: float32 [2, 512, 512], P(None, 'dp'), may hold values from -0.75 to 0.75
- mixer_gain: float32 [2, 512], P(None, 'dp'), may hold values from 0.5 to 1.5
- expand_weight: float32 [2, 512, 2048], P(None, 'dp'), may hold values from -0.25 to 0.25
- reduce_weight: float32 [2, 2048, 512], P(None, 'dp'), may hold values from -0.125 to 0.125
- feed_gain: float32 [2, 512], P(None, 'dp'), may hold values from 0.5 to 1.5
- final_gain: float32 [512], P('dp'), may hold values from 0.5 to 1.5
Outputs:
- item_loss: float32 [32], P('dp')
- logit_grad: float32 [32, 640, 256], P('dp', None, 'section')
- embedding_grad: float32 [512, 256], P('dp', 'section')
- mixer_grad: float32 [2, 512, 1536], P(None, 'dp')
- output_grad: float32 [2, 512, 512], P(None, 'dp')
- mixer_gain_grad: float32 [2, 512], P(None, 'dp')
- expand_grad: float32 [2, 512, 2048], P(None, 'dp')
- reduce_grad: float32 [2, 2048, 512], P(None, 'dp')
- feed_gain_grad: float32 [2, 512], P(None, 'dp')
- final_gain_grad: float32 [512], P('dp')
Inputs may be any that keep to these rules, and one draw needn't show every extreme that they name: `padding_mask`: each item's mask is 1 on its first 320 or more positions and 0 on all positions after them.
All inputs are finite; a program needn't handle non-finite values.
Results may differ from a plain program's by a relative error of at most 0.006.
The roundings to bfloat16 on the way count: a program that leaves them out, or rounds other values in their place, can miss the bound.
Values may be sent and summed in bfloat16 or wider, within the bound.
A program may use at most 192 MiB of HBM per device.

v0:
```python
import functools

import jax
import jax.numpy as jnp
from jax import lax
from jax.experimental import pallas as pl
from jax.experimental.pallas import tpu as pltpu
from jax.sharding import PartitionSpec as P

D = 512
HEADS = 8
HD = 64
FF = 2048
VOCAB = 256
BAND = 30
LEN = 640
LAYERS = 2
CH = 128
CHUNKS = LEN // CH
REACH = 32
WIDE = tuple((t0, min(t0 + 256, LEN)) for t0 in range(0, LEN, 256))
TILE = 512
BACK = 256
F32 = jnp.float32
DP, SECTION = ("dp", "section")
BF16 = jnp.bfloat16


def mm(left, right):
    return jnp.dot(left, right, preferred_element_type=F32)


def mm_nt(left, right):
    return lax.dot_general(left, right, (((1,), (1,)), ((), ())), preferred_element_type=F32)


def norm_forward(v, gain):
    scale = lax.rsqrt(jnp.mean(v * v, axis=-1, keepdims=True) + 1e-05)
    return v * scale * gain


def norm_backward(v, gain, dy):
    scale = lax.rsqrt(jnp.mean(v * v, axis=-1, keepdims=True) + 1e-05)
    normed = v * scale
    dgain = jnp.sum(dy * normed, axis=0, keepdims=True)
    dyg = dy * gain
    dv = scale * (dyg - normed * jnp.mean(dyg * normed, axis=-1, keepdims=True))
    return dv, dgain


def gelu_parts(u):
    c = 0.7978845608028654
    square = u * u
    t = jnp.tanh(u * (c + (c * 0.044715) * square))
    half = 0.5 * (1.0 + t)
    value = u * half
    slope = half + 0.5 * u * (1.0 - t * t) * (c + (3.0 * c * 0.044715) * square)
    return value, slope


def feature_parts(u):
    low_exp = jnp.exp(jnp.minimum(u, 0.0))
    first = jnp.where(u > 0.0, u + 1.0, low_exp)
    second = jnp.tanh(u)
    return first, low_exp, second


def iotas(rows, cols, row0=0):
    r = lax.broadcasted_iota(jnp.int32, (rows, cols), 0) + row0
    c = lax.broadcasted_iota(jnp.int32, (rows, cols), 1)
    return r, c


def near_part(i, key_rows, query_cols):
    row0 = -REACH if i > 0 else 0
    scores = mm(key_rows, query_cols) * 0.125
    r, c = iotas(CH - row0, CH, row0)
    ok = (r <= c) & (c - r < BAND)
    scores = jnp.where(ok, scores, -1e30)
    peak = jnp.max(scores, axis=0, keepdims=True)
    weights = jnp.exp(scores - peak)
    return weights / jnp.sum(weights, axis=0, keepdims=True)


def causal_rows(i, block):
    row0 = -REACH if i > 0 else 0
    r, c = iotas(CH - row0, CH, row0)
    return jnp.where(r <= c, block, 0.0)


START, WAIT = range(2)


def every(copies, act):
    for copy in copies:
        if act == START:
            copy.start()
        else:
            copy.wait()


def halves(t0, t1, half):
    parts = []
    for i in range(t0 // CH, t1 // CH):
        part = half(i)
        if part.shape[0] < t1:
            part = jnp.concatenate([part, jnp.zeros((t1 - part.shape[0], CH), part.dtype)], axis=0)
        parts.append(part)
    return parts[0] if len(parts) == 1 else jnp.concatenate(parts, axis=1)


def first_row(i):
    return i * CH - REACH if i > 0 else 0


def mixture_block(t0, t1, key_nat, key_feat2, query_masked, query_feat2, near_ref):
    far = mm(key_feat2[:t1], query_feat2[:, t0:t1])

    def half(i):
        r0, end = first_row(i), (i + 1) * CH
        near = near_part(i, key_nat[r0:end], query_masked[:, i * CH:end])
        near_ref[i, :end - r0, :] = near
        column = far[:end, i * CH - t0:end - t0]
        bottom = (causal_rows(i, column[r0:]) + near).astype(BF16)
        if r0 == 0:
            return bottom
        return jnp.concatenate([column[:r0].astype(BF16), bottom], axis=0)

    return halves(t0, t1, half)


def query_features(qT, inv1, inv2):
    first, slope1, second = feature_parts(qT.astype(F32))
    first_b, second_b = first.astype(BF16), second.astype(BF16)
    scaled = jnp.concatenate([first_b.astype(F32) * inv1, second_b.astype(F32) * inv2], axis=0)
    high = scaled.astype(BF16)
    rest = (scaled - high.astype(F32)).astype(BF16)
    return first_b, slope1, second, jnp.concatenate([high, rest], axis=0)


def masked_pair(part, e):
    zero = jnp.zeros_like(part)
    return jnp.concatenate([part, zero] if e == 0 else [zero, part], axis=0)


ALL, MINE, MINE_A, MINE_B, OTHER = range(5)


class Links:
    def __init__(self, pieces, send_sem, recv_sem):
        self.pieces, self.send_sem, self.recv_sem = pieces, send_sem, recv_sem
        d, z = lax.axis_index(DP), lax.axis_index(SECTION)
        core, x, y = d % 2, (d // 2) % 2, d // 4
        self.d, self.half = d, z % 2
        self.core_n, self.x_n, self.y_n, self.z_n = d + 1 - 2 * core, d + 2 - 4 * x, d + 4 - 8 * y, z + 1 - 2 * (z % 2)
        self.diag = self.x_n + 4 - 8 * y

    def columns(self, n, part):
        _, _, cols, cut, shared = self.pieces[n]
        if part == ALL or (part == MINE and not shared):
            return slice(None)
        if not shared:
            return slice(0, cut) if part == MINE_A else slice(cut, cols)
        half, quarter = cols // 2, cols // 4
        start = half * (1 - self.half if part == OTHER else self.half) + (quarter if part == MINE_B else 0)
        return pl.ds(pl.multiple_of(start, quarter), quarter if part in (MINE_A, MINE_B) else half)

    def copy(self, n, kind):
        ref, rows = self.pieces[n][:2]
        core, x, y, z = {DP: self.core_n}, {DP: self.x_n}, {DP: self.y_n}, {SECTION: self.z_n}
        block, part, target = (
            (self.d, MINE, x),
            (self.d, MINE, y),
            (self.y_n, MINE_A, x),
            (self.x_n, MINE_B, y),
            (self.d, ALL, core),
            (self.x_n, MINE, core),
            (self.y_n, MINE, core),
            (self.diag, MINE_A, core),
            (self.diag, MINE_B, core),
            (self.x_n, MINE, z),
            (self.y_n, MINE, z),
            (self.diag, MINE, z),
            (self.x_n, OTHER, core),
            (self.y_n, OTHER, core),
            (self.diag, OTHER, core),
        )[kind]
        view = ref.at[pl.ds(pl.multiple_of(block * rows, rows), rows), self.columns(n, part)]
        return pltpu.make_async_remote_copy(
            src_ref=view, dst_ref=view, send_sem=self.send_sem.at[n, kind], recv_sem=self.recv_sem.at[n, kind],
            device_id=target, device_id_type=pl.DeviceIdType.MESH,
        )

    def own(self, *ns):
        for n in ns:
            for kind in (0, 1, 4):
                self.copy(n, kind).start()

    def first(self, *ns):
        for n in ns:
            shared = self.pieces[n][4]
            self.copy(n, 0).wait_recv()
            self.copy(n, 3).start()
            self.copy(n, 1).wait_recv()
            self.copy(n, 2).start()
            for kind in (9, 10, 5, 6) if shared else (5, 6):
                self.copy(n, kind).start()

    def second(self, *ns):
        for n in ns:
            shared = self.pieces[n][4]
            self.copy(n, 2).wait_recv()
            self.copy(n, 7).start()
            self.copy(n, 3).wait_recv()
            for kind in (11, 8) if shared else (8,):
                self.copy(n, kind).start()

    def third(self, *ns):
        for n in ns:
            for kind in (9, 10, 11):
                self.copy(n, kind).wait_recv()
                self.copy(n, kind + 3).start()

    def ready(self, *ns):
        for n in ns:
            for kind in (4, 5, 6, 7, 8) + ((12, 13, 14) if self.pieces[n][4] else ()):
                self.copy(n, kind).wait_recv()

    def finish(self):
        for n, piece in enumerate(self.pieces):
            for kind in range(15 if piece[4] else 9):
                self.copy(n, kind).wait_send()


class Sums:
    def __init__(self, links, pieces, send_sem, recv_sem, tile_send, tile_recv):
        self.links, self.pieces, self.send_sem, self.recv_sem = links, pieces, send_sem, recv_sem
        self.tile_send, self.tile_recv = tile_send, tile_recv
        d = links.d
        self.core, self.x, self.y = d % 2, (d // 2) % 2, d // 4
        self.z = lax.axis_index(SECTION)
        self.inner = (self.z == 1) | (self.z == 2)
        self.outer = (self.z == 0) | (self.z == 3)

    def view(self, piece, ref, block, count, half=None):
        blocks = pl.ds(pl.multiple_of(block * piece.size, piece.size), count * piece.size)
        across = {None: slice(None), 0: slice(0, piece.split), 1: slice(piece.split, piece.across)}[half]
        return ref.at[across, blocks] if piece.by_columns else ref.at[blocks, across]

    def tile_copy(self, block):
        r = self.pieces[R0]
        src = r.whole.at[:, pl.ds(pl.multiple_of((4 * (1 - self.core) + block) * r.size, r.size), r.size)]
        dst = r.whole_r1.at[:, pl.ds(pl.multiple_of(block * r.size, r.size), r.size)]
        return pltpu.make_async_remote_copy(
            src_ref=src, dst_ref=dst, send_sem=self.tile_send.at[block], recv_sem=self.tile_recv.at[block],
            device_id={DP: self.links.core_n}, device_id_type=pl.DeviceIdType.MESH,
        )

    def copy(self, name, kind, l=None):
        piece = self.pieces[name]
        core, x, y, z, links = self.core, self.x, self.y, self.z, self.links
        mine = 4 * core

        def pair(block, to, at, count, half):
            return self.view(piece, piece.grad, block, count, half), self.view(piece, to, at, count, half)

        if kind == 0:
            src, dst = pair(4 * (1 - core), piece.r1, 0, 4, None)
        elif kind in (1, 2):
            src, dst = pair(mine + 2 * (kind - 1) + 1 - x, piece.r2, kind - 1, 1, 0)
        elif kind == 3:
            src, dst = pair(mine + 2 * (1 - y), piece.r2, 0, 2, 1)
        elif kind == 4:
            src, dst = pair(mine + 2 * (1 - y) + x, piece.r3, 0, 1, 0)
        elif kind == 5:
            src, dst = pair(mine + 2 * y + 1 - x, piece.r3, 0, 1, 1)
        else:
            src = piece.r3
            dst = piece.rz.at[kind - 6] if kind < 8 else piece.out(l)
        device = (
            {DP: links.core_n}, {DP: links.x_n}, {DP: links.x_n}, {DP: links.y_n}, {DP: links.y_n}, {DP: links.x_n},
            {SECTION: z + 1 - 2 * (z // 3)}, {SECTION: 3 - z}, {SECTION: 3 * (z // 2)},
        )[kind]
        return pltpu.make_async_remote_copy(
            src_ref=src, dst_ref=dst, send_sem=self.send_sem.at[piece.index, kind], recv_sem=self.recv_sem.at[piece.index, kind],
            device_id=device, device_id_type=pl.DeviceIdType.MESH,
        )

    def add(self, into, other):
        into[...] = (into[...].astype(F32) + other[...].astype(F32)).astype(BF16)

    def step(self, name, number, l):
        piece = self.pieces[name]
        grad, r1, r2, r3, rz = piece.grad, piece.r1, piece.r2, piece.r3, piece.rz
        mine = 4 * self.core
        own = mine + 2 * self.y + self.x
        tiles = name in (R0, R1)
        if number == 1:
            self.copy(name, 0).start()
        elif number == 2:
            if not tiles:
                self.copy(name, 0).wait_recv()
            elif name == R0:
                for block in range(4):
                    self.tile_copy(block).wait_recv()
            self.add(self.view(piece, grad, mine, 4), self.view(piece, r1, 0, 4))
            for kind in (1, 2, 3):
                self.copy(name, kind).start()
        elif number == 3:
            for kind in (1, 2):
                self.copy(name, kind).wait_recv()
                self.add(self.view(piece, grad, mine + 2 * (kind - 1) + self.x, 1, 0), self.view(piece, r2, kind - 1, 1, 0))
            self.copy(name, 3).wait_recv()
            self.copy(name, 4).start()
            self.add(self.view(piece, grad, mine + 2 * self.y, 2, 1), self.view(piece, r2, 0, 2, 1))
            self.copy(name, 5).start()
        elif number == 4:
            for half in (0, 1):
                self.copy(name, 4 + half).wait_recv()
                self.add(self.view(piece, r3, 0, 1, half), self.view(piece, grad, own, 1, half))

            @pl.when(self.outer)
            def _():
                self.copy(name, 6).start()

            if not tiles:
                self.copy(name, 0).wait_send()
            elif name == R0:
                for block in range(4):
                    self.tile_copy(block).wait_send()
            for kind in range(1, 6):
                self.copy(name, kind).wait_send()
        elif number == 5:

            @pl.when(self.inner)
            def _():
                self.copy(name, 6).wait_recv()
                self.add(r3, rz.at[0])
                self.copy(name, 7).start()
        elif number == 6:

            @pl.when(self.inner)
            def _():
                self.copy(name, 7).wait()
                self.add(r3, rz.at[1])
                self.copy(name, 8, l).start()
                self.local(piece, l).start()
        elif number == 7:

            @pl.when(self.outer)
            def _():
                self.copy(name, 6).wait_send()
                self.copy(name, 8, l).wait_recv()

            @pl.when(self.inner)
            def _():
                self.copy(name, 8, l).wait_send()
                self.local(piece, l).wait()

    def local(self, piece, l):
        return pltpu.make_async_copy(piece.r3, piece.out(l), self.send_sem.at[piece.index, 9])


class Piece:
    def __init__(self, index, refs, size, across, split, out, by_columns=False, whole=None):
        self.index, self.size, self.across, self.split, self.out, self.by_columns = index, size, across, split, out, by_columns
        self.grad, self.r1, self.r2, self.r3, self.rz = refs
        self.whole, self.whole_r1 = whole or (None, None)


def sum_pieces(refs, out_m, out_o, out_e, out_r, out_t):
    def part(n, index):
        return [refs[name + n].at[index] for name in ("grad_", "r1", "r2", "r3")] + [refs["rz" + n].at[(slice(None),) + index]]

    every = slice(None)
    pieces = {}
    for i in range(2):
        cols = slice(FF // 2 * i, FF // 2 * (i + 1))
        pieces[E0 + i] = Piece(E0 + i, part("e", (every, cols)), 64, FF // 2, FF // 4, lambda l, cols=cols: out_e.at[l, :, cols])
    for i in range(2):
        rows = slice(D // 2 * i, D // 2 * (i + 1))
        pieces[R0 + i] = Piece(
            R0 + i, part("r", (rows, every)), 256, D // 2, D // 4, lambda l, rows=rows: out_r.at[l, rows], True,
            (refs["grad_r"], refs["r1r"]),
        )
    for i in range(4):
        cols = slice(384 * i, 384 * (i + 1))
        pieces[M0 + i] = Piece(
            M0 + i, part("m", (every, cols)), 64, 384, 128 * (1 + i % 2), lambda l, i=i: out_m.at[l, i]
        )
    pieces[O] = Piece(O, part("o", (every, every)), 64, D, D // 2, lambda l: out_o.at[l])
    pieces[T] = Piece(T, part("t", (every, every)), 64, 384, 128, lambda l: out_t)
    return pieces


def by_position(rows):
    size = rows.shape[0] // 8
    return jnp.concatenate([rows[size * i:size * (i + 1)] for i in (0, 2, 4, 6, 1, 3, 5, 7)], axis=0)


def step_kernel(linked, *refs):
    names = (LINKED_IN + LINKED_OUT) if linked else (PLAIN_IN + PLAIN_OUT)
    names += tuple(SCRATCH) + tuple(LINKED_SCRATCH if linked else PLAIN_SCRATCH)
    step_body(linked, **dict(zip(names, refs, strict=True)))


def step_body(
    linked, loss, lg, kept_m, kept_near, x, x1, dx, kv, pT, inv1s, cum, oT, hT, g, gT, wide, a1k, m, near, keep_sem, d, ds, doT, dpT, yb, acc,
    columns=None, table=None, gm=None, gf=None, gz=None, wm=None, wo=None, we=None, wr=None, stage=None, stage_half=None, sem=None, sem_half=None,
    dtable=None, dgm=None, dgf=None, dgz=None, dwm=None, dwo=None, dwe=None, dwrt=None,
    tokens=None, mask=None, emb=None, mgain=None, fgain=None, zgain=None, wm_s=None, wo_s=None, we_s=None, wr_s=None, tz=None, gains=None, lgs=None, losss=None,
    send_sem=None, recv_sem=None, zsend=None, zrecv=None, load_sem=None, sum_send=None, sum_recv=None, tile_send=None, tile_recv=None,
    out_m=None, out_o=None, out_e=None, out_r=None, out_t=None, dgains=None, **sums_refs,
):
    table_ref = table
    gm_ref, gf_ref, gz_ref = gm, gf, gz
    wm_ref, wo_ref, we_ref, wr_ref = wm, wo, we, wr
    loss_ref, lg_ref, dtable_ref, dgm_ref, dgf_ref, dgz_ref = loss, lg, dtable, dgm, dgf, dgz
    dwm_ref, dwo_ref, dwe_ref, dwrt_ref = dwm, dwo, dwe, dwrt
    x_ref, x1_ref, dx_ref, kv_ref, pT_ref, inv1_ref, cum_ref = x, x1, dx, kv, pT, inv1s, cum
    oT_ref, hT_ref, g_ref, gT_ref, wide_ref, a1k_ref, near_ref, m_ref, d_ref, ds_ref = oT, hT, g, gT, wide, a1k, near, m, d, ds
    doT_ref, dpT_ref, w_ref, yb_ref, acc_ref = doT, dpT, a1k, yb, acc
    xs = [x_ref.at[0], x_ref.at[1], dx_ref]
    placed = by_position if linked else (lambda rows: rows)
    r, c = iotas(LEN, LEN)
    upper = (r <= c).astype(F32).astype(BF16)

    if linked:
        zi = lax.axis_index(SECTION)
        links = Links(
            [(table_ref, 64, 384, 256, False)]
            + [
                entry
                for l in range(LAYERS)
                for entry in (
                    (wm_ref.at[l], 64, 3 * D, 3 * D // 2, SHARED[l][0]),
                    (wo_ref.at[l], 64, D, D // 2, SHARED[l][1]),
                    (we_ref.at[l], 64, FF, FF // 2, SHARED[l][2]),
                    (wr_ref.at[l], 256, D, D // 2, SHARED[l][3]),
                )
            ],
            send_sem, recv_sem,
        )

        def along_z(n, k, src_of, dst):
            target = (zi + k) % 4
            return pltpu.make_async_remote_copy(
                src_ref=src_of(target), dst_ref=dst.at[zi], send_sem=zsend.at[n, k - 1], recv_sem=zrecv.at[n, k - 1],
                device_id={SECTION: target}, device_id_type=pl.DeviceIdType.MESH,
            )

        def table_copy(k):
            return along_z(0, k, lambda target: tz.at[zi], tz)

        def lg_copy(k):
            return along_z(1, k, lambda target: lgs.at[target], lg_ref)

        def loss_copy(k):
            return along_z(2, k, lambda target: losss, loss_ref)

        loads = []
        for l in range(LAYERS):
            pairs = [(wm_s.at[l, :, TILE * j:TILE * (j + 1)], x1_ref.at[l, 64 * j:64 * (j + 1)]) for j in range(3)]
            pairs += [(wo_s.at[l], x1_ref.at[l, 192:256])]
            pairs += [(we_s.at[l, :, TILE * j:TILE * (j + 1)], x1_ref.at[l, 256 + 64 * j:320 + 64 * j]) for j in range(4)]
            pairs += [(wr_s.at[l], x_ref.at[1, 256 * l:256 * (l + 1)])]
            loads.append([pltpu.make_async_copy(src, dst, load_sem.at[l, i]) for i, (src, dst) in enumerate(pairs)])
            for load in loads[l]:
                load.start()

        def take(l, part):
            for i in {"m": (0, 1, 2), "o": (3,), "e": (4, 5, 6, 7), "r": (8,)}[part]:
                loads[l][i].wait()
            if part == "m":
                for j in range(3):
                    wm_ref[l, own64, TILE * j:TILE * (j + 1)] = x1_ref[l, 64 * j:64 * (j + 1)].astype(BF16)
            elif part == "o":
                wo_ref[l, own64] = x1_ref[l, 192:256].astype(BF16)
            elif part == "e":
                for j in range(4):
                    we_ref[l, own64, TILE * j:TILE * (j + 1)] = x1_ref[l, 256 + 64 * j:320 + 64 * j].astype(BF16)
            else:
                wr_ref[l, own256] = x_ref[1, 256 * l:256 * (l + 1)].astype(BF16)

        barrier = pltpu.get_barrier_semaphore()
        for target in (links.core_n, links.x_n, links.y_n):
            pl.semaphore_signal(barrier, inc=1, device_id={DP: target}, device_id_type=pl.DeviceIdType.MESH)
        for k in (1, 2, 3):
            pl.semaphore_signal(barrier, inc=1, device_id={SECTION: (zi + k) % 4}, device_id_type=pl.DeviceIdType.MESH)
        pl.semaphore_wait(barrier, 6)

        own64 = pl.ds(pl.multiple_of(links.d * 64, 64), 64)
        own256 = pl.ds(pl.multiple_of(links.d * 256, 256), 256)
        r, _ = iotas(8, 64)
        rows = [mgain[0:1], mgain[1:2], fgain[0:1], fgain[1:2], zgain[0:1]]
        gathered = sum(jnp.where(r == i, row, 0.0) for i, row in enumerate(rows))
        gathered = jnp.concatenate([gathered, jnp.zeros((8, 64), F32)], axis=1)
        gathered = jnp.concatenate([gathered, jnp.zeros((120, 128), F32)], axis=0).T[:64]
        small_b = (jnp.concatenate([emb[...], jnp.zeros((64, 64), F32)], axis=1) + pltpu.roll(gathered, 64, 1)).astype(BF16)
        tz[zi] = small_b
        for k in (1, 2, 3):
            table_copy(k).start()
        take(0, "m")
        links.own(1)
        r, c = iotas(8, LEN)
        ids = tokens[pl.ds(zi, 1), :].astype(F32)
        scored = mask[pl.ds(zi, 1), :].astype(F32)
        rows = [ids, pltpu.roll(ids, LEN - 1, 1), pltpu.roll(scored, LEN - 1, 1)]
        rows = sum(jnp.where((r == i) & ((c < LEN - 1) | (r == 0)), row, 0.0) for i, row in enumerate(rows))
        columns[...] = rows.T.astype(jnp.int32)
        take(0, "o")
        for k in (1, 2, 3):
            table_copy(k).wait_recv()
        pad = jnp.zeros((64, 64), BF16)
        table_ref[own64, :] = jnp.concatenate([tz[i][:, :64] for i in range(4)] + [small_b[:, 64:], pad], axis=1)
        links.own(0, 2)
        take(0, "e")
        wide_ref[...] = upper
        links.first(1, 0)
        links.own(3)
        links.first(2)
        take(0, "r")
        links.own(4)
        for part in "moer":
            take(1, part)
        links.second(1, 0)
        links.ready(0)
        gains[...] = table_ref[:, 256:].astype(F32).T[:8]
        table_ref = table_ref.at[:, :256]
        gm_ref, gf_ref, gz_ref = [gains[i:i + 1] for i in range(2)], [gains[i:i + 1] for i in range(2, 4)], gains[4:5]
        sums = Sums(
            links, sum_pieces(sums_refs, out_m, out_o, out_e, out_r, out_t), sum_send, sum_recv, tile_send, tile_recv
        )
    else:
        wide_ref[...] = upper
        gm_ref, gf_ref, gz_ref = [gm_ref[i] for i in range(2)], [gf_ref[i] for i in range(2)], gz_ref[...]

    def service(step, index=None, only=lambda at: True):
        if not linked:
            return
        for at, acts in SERVICE.get(step, {}).items():
            if not only(at):
                continue

            def run(acts=acts):
                for act in acts:
                    if isinstance(act[0], int):
                        sums.step(*act)
                    else:
                        act[0](links, *act[1:])

            if at is None:
                run()
            else:
                pl.when(index == at)(run)

    inv2 = 1.0 / (lax.broadcasted_iota(jnp.int32, (1, LEN), 1).astype(F32) + 1.0)

    def emit(slot, wait_first, value, dst):
        into, sems = (stage, sem) if dst.shape[1] == TILE else (stage_half, sem_half)

        def copy():
            return pltpu.make_async_copy(into.at[slot], dst, sems.at[slot])

        if wait_first is True:
            copy().wait()
        elif wait_first is not False:
            pl.when(wait_first)(lambda: copy().wait())
        into[slot] = value.astype(BF16)
        copy().start()

    def put_gain(row, value):
        if linked:
            dgains[row:row + 1] = value
        elif row < 2:
            dgm_ref[row] = value
        elif row < 4:
            dgf_ref[row - 2] = value
        else:
            dgz_ref[...] = value

    def by_rows(run, init=None):
        def some(i, carry):
            return run(pl.ds(pl.multiple_of(i * CH, CH), CH), carry)

        return lax.fori_loop(0, CHUNKS, some, init)

    def normed_rows(src, gain, dst, dstT):
        def some(rows, carry):
            block = norm_forward(src[rows], gain).astype(BF16)
            dst[rows] = block
            dstT[:, rows] = placed(block.T)
            return carry

        by_rows(some, 0)

    def back_rows(src, gain, row):
        def some(rows, dgain):
            dv, dg = norm_backward(src[rows], gain, acc_ref[rows])
            dx_ref[rows] += dv
            return dgain + dg

        put_gain(row, by_rows(some, jnp.zeros((1, D), F32)))

    vocab_ids = lax.broadcasted_iota(jnp.int32, (LEN, VOCAB), 1)
    hot = (vocab_ids == columns[:, 0:1]).astype(F32).astype(BF16)
    x_ref[0] = mm_nt(hot, table_ref[...])
    if linked:
        links.ready(1)

    def keep(l, h, e):
        return (
            pltpu.make_async_copy(m_ref.at[e], kept_m.at[l, h], keep_sem.at[e, 0]),
            pltpu.make_async_copy(near_ref.at[e], kept_near.at[l, h], keep_sem.at[e, 1]),
        )

    def fetch(l, h, e):
        return (
            pltpu.make_async_copy(kept_m.at[l, h], m_ref.at[e], keep_sem.at[e, 0]),
            pltpu.make_async_copy(kept_near.at[l, h], near_ref.at[e], keep_sem.at[e, 1]),
        )

    m_ref[...] = jnp.zeros_like(m_ref)
    near_ref[...] = jnp.zeros_like(near_ref)

    def attention_forward(l):
        normed_rows(x_ref.at[l], gm_ref[l], yb_ref, hT_ref.at[l])
        h = yb_ref[...]
        for j in range(3):
            part = mm(h, wm_ref[l, :, j * TILE:(j + 1) * TILE]).astype(BF16)
            if j > 0:
                kv_ref[l, :, (j - 1) * TILE:j * TILE] = part
            pT_ref[l, j * TILE:(j + 1) * TILE, :] = part.T
        service((MIXER, l))
        kT = pT_ref[l, D:2 * D, :].astype(F32)
        a1k_ref[...] = feature_parts(kT)[0].astype(BF16)
        for i in range(CHUNKS):
            t0, t1 = i * CH, (i + 1) * CH
            cum_ref[l, :, t0:t1] = mm(a1k_ref[:, :t1], wide_ref[:t1, t0:t1])

        def pair(p, carry):
            base = pl.multiple_of(p * CH, CH)
            for e in range(2):
                row = pl.multiple_of(base + e * HD, HD)
                if l == 0:
                    pl.when(p > 0)(lambda: every(keep(l, 0, e), WAIT))
                else:
                    for copy in keep(l, 0, e):
                        copy.wait()
                qT = pT_ref[l, pl.ds(row, HD), :]
                kT = pT_ref[l, pl.ds(pl.multiple_of(D + row, HD), HD), :]
                vT = pT_ref[l, pl.ds(pl.multiple_of(2 * D + row, HD), HD), :]
                first_k, _, second_k = feature_parts(kT.astype(F32))
                key_feat = jnp.concatenate([first_k.astype(BF16), second_k.astype(BF16)], axis=0).T
                first_q = feature_parts(qT.astype(F32))[0].astype(BF16).astype(F32)
                total = jnp.sum(first_q * cum_ref[l, pl.ds(row, HD), :], axis=0, keepdims=True)
                inv1 = 1.0 / (total + 1.0)
                inv1_ref[l, 2 * p + e] = inv1
                query_feat2 = query_features(qT, inv1, inv2)[3]
                key_feat2 = jnp.concatenate([key_feat, key_feat], axis=1)
                key_nat = kv_ref[l, :, pl.ds(base, CH)]
                query_masked = masked_pair(qT, e)
                for t0, t1 in WIDE:
                    mixture = mixture_block(t0, t1, key_nat, key_feat2, query_masked, query_feat2, near_ref.at[e])
                    m_ref[e, :t1, t0:t1] = mixture
                    oT_ref[l, pl.ds(row, HD), t0:t1] = mm(vT[:, :t1], mixture).astype(BF16)
                for copy in keep(l, 2 * p + e, e):
                    copy.start()
                service((HEAD, l), 2 * p + e, lambda at: at % 2 == e)
            return carry

        lax.fori_loop(0, HEADS // 2, pair, 0)
        service((OUTPUT, l))
        o = oT_ref[l].T
        x1_ref[l] = x_ref[l] + mm(o, wo_ref[l])

    def feed_forward(l):
        normed_rows(x1_ref.at[l], gf_ref[l], g_ref, gT_ref.at[l])
        xs[l + 1][...] = x1_ref[l]
        service((FEED, l))

        def tile(j, carry):
            col = pl.multiple_of(j * BACK, BACK)
            active = gelu_parts(mm(g_ref[...], we_ref[l, :, pl.ds(col, BACK)]))[0].astype(BF16)
            service((GELU, l), j)
            xs[l + 1][...] += mm(active, wr_ref[l, pl.ds(col, BACK), :])
            service((FEED_TILE, l), j)
            return carry

        lax.fori_loop(0, FF // BACK, tile, 0)

    def head():
        zT_ref, grad_ref = doT_ref, yb_ref.at[:, :VOCAB]

        def some(rows, carry):
            dgain, cross_sum, val_sum = carry
            x = dx_ref[rows]
            z = norm_forward(x, gz_ref).astype(BF16)
            zT_ref[:, rows] = placed(z.T)
            logits = mm(z, table_ref[...])
            ids = lax.broadcasted_iota(jnp.int32, (CH, VOCAB), 1)
            tgt_hot = (ids == columns[rows, 1:2]).astype(F32)
            val = columns[rows, 2:3].astype(F32)
            peak = jnp.max(logits, axis=-1, keepdims=True)
            grown = jnp.exp(logits - peak)
            total = jnp.sum(grown, axis=-1, keepdims=True)
            lse = peak + jnp.log(total)
            picked = jnp.sum(logits * tgt_hot, axis=-1, keepdims=True)
            cross = (lse - picked) * val
            grad_b = ((grown / total - tgt_hot) * val).astype(BF16)
            grad_ref[rows, :] = grad_b
            if linked:
                grad_bT = grad_b.T
                for i in range(4):
                    lgs[i, :, rows] = grad_bT[64 * i:64 * i + 64]
            else:
                lg_ref[rows, :] = grad_b
            dv, dg = norm_backward(x, gz_ref, mm_nt(grad_b, table_ref[...]))
            dx_ref[rows] = dv
            return (
                dgain + dg,
                cross_sum + jnp.sum(cross, axis=0, keepdims=True),
                val_sum + jnp.sum(val, axis=0, keepdims=True),
            )

        nothing = jnp.zeros((1, 1), F32)
        dgain, cross_sum, val_sum = by_rows(some, (jnp.zeros((1, D), F32), nothing, nothing))
        put_gain(4, dgain)
        loss = jnp.broadcast_to(cross_sum / val_sum, (8, 128))
        if linked:
            losss[...] = loss
            for k in (1, 2, 3):
                lg_copy(k).start()
                loss_copy(k).start()
            pltpu.make_async_copy(lgs.at[zi], lg_ref.at[zi], zsend.at[1, 3]).start()
            pltpu.make_async_copy(losss, loss_ref.at[zi], zsend.at[2, 3]).start()
        else:
            loss_ref[...] = loss
        dtable_ref[...] = mm(zT_ref[...], grad_ref[...])

    def feed_backward(l):
        def some(rows, carry):
            yb = dx_ref[rows].astype(BF16)
            yb_ref[rows] = yb
            doT_ref[:, rows] = yb.T
            if l < LAYERS - 1:
                g_ref[rows] = norm_forward(x1_ref[l, rows], gf_ref[l]).astype(BF16)
            return carry

        by_rows(some, 0)
        acc_ref[...] = jnp.zeros_like(acc_ref)

        def tile(j, carry):
            col = pl.multiple_of(j * BACK, BACK)
            slot = lax.rem(j, 2)
            later = (j >= 2) if l == LAYERS - 1 else True
            value, slope = gelu_parts(mm(g_ref[...], we_ref[l, :, pl.ds(col, BACK)]))
            dreduce = mm(doT_ref[...], value.astype(BF16))
            if linked:
                place = pl.multiple_of(BACK * (lax.rem(j, 2) * 4 + lax.div(j, 2)), BACK)
                sums_refs["grad_r"][:, pl.ds(place, BACK)] = dreduce.astype(BF16)
                pl.when(lax.rem(j, 2) != sums.core)(lambda: sums.tile_copy(lax.div(j, 2)).start())
            else:
                emit(slot, later, dreduce, dwrt_ref.at[l, :, pl.ds(col, BACK)])
            dact = mm_nt(yb_ref[...], wr_ref[l, pl.ds(col, BACK), :])
            dhid = (dact * slope).astype(BF16)
            dexpand = mm(gT_ref[l], dhid)
            if linked:
                sums_refs["grad_e"][:, pl.ds(col, BACK)] = dexpand.astype(BF16)
            else:
                emit(2 + slot, later, dexpand, dwe_ref.at[l, :, pl.ds(col, BACK)])
            dnormed = mm_nt(dhid, we_ref[l, :, pl.ds(col, BACK)])

            acc_ref[...] += dnormed
            service((BACK_TILE, l), j)
            return carry

        lax.fori_loop(0, FF // BACK, tile, 0)
        service((BACK_FEED, l))
        back_rows(x1_ref.at[l], gf_ref[l], 2 + l)

    def attention_backward(l):
        yb_ref[...] = dx_ref[...].astype(BF16)
        yb = yb_ref[...]
        doutput = mm(placed(oT_ref[l]), yb)
        if linked:
            sums_refs["grad_o"][...] = doutput.astype(BF16)
        else:
            emit(0, l < LAYERS - 1, doutput, dwo_ref.at[l])
        service((BACK_OUTPUT, l))
        doT_ref[...] = mm_nt(yb, wo_ref[l]).astype(BF16).T

        for e in range(2):
            for copy in fetch(l, e, e):
                copy.start()

        def pair(p, carry):
            base = pl.multiple_of(p * CH, CH)
            for e in range(2):
                row = pl.multiple_of(base + e * HD, HD)
                qT = pT_ref[l, pl.ds(row, HD), :]
                kT = pT_ref[l, pl.ds(pl.multiple_of(D + row, HD), HD), :]
                doT = doT_ref[pl.ds(row, HD), :]
                inv1 = inv1_ref[l, 2 * p + e]
                first_q, slope1_q, second_q, query_feat2 = query_features(qT, inv1, inv2)
                first_k, slope1_k, second_k = feature_parts(kT.astype(F32))
                key_featT = jnp.concatenate([first_k.astype(BF16), second_k.astype(BF16)], axis=0)
                value_nat = kv_ref[l, :, pl.ds(pl.multiple_of(D + base, CH), CH)]
                do_masked = masked_pair(doT, e)
                for copy in fetch(l, 2 * p + e, e):
                    copy.wait()
                far_q, near_q = [], []
                for t0, t1 in WIDE:
                    dm = mm(value_nat[:t1], do_masked[:, t0:t1])

                    def half(i):
                        r0, end = first_row(i), (i + 1) * CH
                        column = dm[:end, i * CH - t0:end - t0]
                        bottom = column[r0:]
                        near = near_ref[e, i, :end - r0, :]
                        weighted = near * bottom
                        dsum = jnp.sum(weighted, axis=0, keepdims=True)
                        ds = ((weighted - near * dsum) * 0.125).astype(BF16)
                        if i > 0:
                            before = jnp.concatenate([jnp.zeros((CH - REACH, CH), BF16), ds[:REACH]], axis=0)
                            ds_ref[end - 2 * CH:end - CH, CH:] = before
                            ds = ds[REACH:]
                            near_q.append(mm(kT[:, end - 2 * CH:end], jnp.concatenate([before, ds], axis=0)))
                        else:
                            near_q.append(mm(kT[:, :end], ds))
                        ds_ref[end - CH:end, :CH] = ds
                        lower = causal_rows(i, bottom).astype(BF16)
                        if r0 == 0:
                            return lower
                        return jnp.concatenate([column[:r0].astype(BF16), lower], axis=0)

                    dm_b = halves(t0, t1, half)
                    d_ref[:t1, t0:t1] = dm_b
                    far_q.append(mm(key_featT[:, :t1], dm_b))
                farT = jnp.concatenate(far_q, axis=1)
                y1, y2 = farT[:HD], farT[HD:]
                first_qf = first_q.astype(F32)
                m = inv1 * jnp.sum(first_qf * y1, axis=0, keepdims=True)
                cum = cum_ref[l, pl.ds(row, HD), :]
                dq = jnp.concatenate(near_q, axis=1)
                dq = dq + (inv1 * (y1 - m * cum)) * slope1_q + (inv2 * y2) * (1.0 - second_q * second_q)
                dpT_ref[pl.ds(row, HD), :] = dq.astype(BF16)
                w_ref[pl.ds(row, HD), :] = (first_qf * (m * inv1)).astype(BF16)
                for t0, t1 in WIDE:
                    far = mm_nt(query_feat2[:CH, t0:], d_ref[t0:t1, t0:])
                    back = mm_nt(w_ref[pl.ds(row, HD), t0:], wide_ref[t0:t1, t0:])
                    near_k = []
                    for u0 in range(t0, t1, CH):
                        u2 = min(u0 + 2 * CH, LEN)
                        near_k.append(mm_nt(qT[:, u0:u2], ds_ref[u0:u0 + CH, :u2 - u0]))
                    near = near_k[0] if len(near_k) == 1 else jnp.concatenate(near_k, axis=1)
                    dk = near + (far[:HD] - back) * slope1_k[:, t0:t1]
                    dk = dk + far[HD:] * (1.0 - second_k[:, t0:t1] * second_k[:, t0:t1])
                    dpT_ref[pl.ds(pl.multiple_of(D + row, HD), HD), t0:t1] = dk.astype(BF16)
                    dv = mm_nt(doT[:, t0:], m_ref[e, t0:t1, t0:])
                    dpT_ref[pl.ds(pl.multiple_of(2 * D + row, HD), HD), t0:t1] = dv.astype(BF16)
                pl.when(p < HEADS // 2 - 1)(lambda: every(fetch(l, 2 * p + e + 2, e), START))
                service((BACK_HEAD, l), 2 * p + e, lambda at: at % 2 == e)
            if linked:
                for j in range(3):
                    block = mm_nt(hT_ref[l], dpT_ref[pl.ds(pl.multiple_of(j * D + base, CH), CH), :])
                    place = pl.multiple_of(3 * base + j * CH, CH)
                    sums_refs["grad_m"][:, pl.ds(place, CH)] = block.astype(BF16)
                service((BACK_PAIR, l), p)
            return carry

        lax.fori_loop(0, HEADS // 2, pair, 0)
        if not linked:
            for j in range(3):
                block = mm_nt(hT_ref[l], dpT_ref[j * TILE:(j + 1) * TILE, :])
                emit(1 + j, l < LAYERS - 1, block, dwm_ref.at[l, :, j * TILE:(j + 1) * TILE])
        for t0 in range(0, LEN, 256):
            t1 = min(t0 + 256, LEN)
            acc_ref[t0:t1] = mm(wm_ref[l], dpT_ref[:, t0:t1]).T
        service((BACK_MIXER, l))
        back_rows(x_ref.at[l], gm_ref[l], l)
        service((BACK_LAYER, l))

    for l in range(LAYERS):
        service((LAYER, l))
        attention_forward(l)
        feed_forward(l)
    for e in range(2):
        for copy in keep(0, 0, e):
            copy.wait()
    head()
    for l in reversed(range(LAYERS)):
        feed_backward(l)
        attention_backward(l)
    dtable_sum = dtable_ref[...] + mm(placed(dx_ref[...].astype(BF16).T), hot)
    if linked:
        sums_refs["grad_t"][:, :VOCAB] = dtable_sum.astype(BF16)
        sums_refs["grad_t"][:, VOCAB:] = placed(jnp.concatenate([dgains[...], jnp.zeros((120, D), F32)], axis=0).T).astype(BF16)
        service((END, 0))
        for k in (1, 2, 3):
            table_copy(k).wait_send()
            lg_copy(k).wait()
            loss_copy(k).wait()
        pltpu.make_async_copy(lgs.at[zi], lg_ref.at[zi], zsend.at[1, 3]).wait()
        pltpu.make_async_copy(losss, loss_ref.at[zi], zsend.at[2, 3]).wait()
        links.finish()
    else:
        dtable_ref[...] = dtable_sum
        for slot in range(4):
            pltpu.make_async_copy(stage.at[slot], dwo_ref.at[0], sem.at[slot]).wait()
            pltpu.make_async_copy(stage_half.at[slot], dwe_ref.at[0, :, :BACK], sem_half.at[slot]).wait()


E0, E1, R0, R1, M0, M1, M2, M3, O, T = range(10)
MIXER, HEAD, FEED, GELU, FEED_TILE, LAYER, BACK_TILE, BACK_FEED, BACK_OUTPUT, BACK_HEAD, BACK_PAIR, BACK_MIXER, BACK_LAYER, END, OUTPUT = range(15)
SHARED = ((False, False, True, False), (False, False, True, False))
SERVICE = {
    (MIXER, 0): {
        None: ((Links.second, 2), (Links.first, 3),),
    },
    (HEAD, 0): {
        0: ((Links.own, 5),),
        4: ((Links.first, 4),),
        5: ((Links.second, 3),),
        7: ((Links.own, 6),),
    },
    (OUTPUT, 0): {
        None: ((Links.ready, 2),),
    },
    (FEED, 0): {
        None: ((Links.own, 7), (Links.third, 3), (Links.ready, 3),),
    },
    (GELU, 0): {
        0: ((Links.second, 4), (Links.ready, 4),),
    },
    (FEED_TILE, 0): {
        0: ((Links.first, 5), (Links.first, 6), (Links.own, 8),),
        5: ((Links.first, 7),),
    },
    (LAYER, 1): {
        None: ((Links.second, 5), (Links.ready, 5),),
    },
    (MIXER, 1): {
        None: ((Links.second, 6),),
    },
    (HEAD, 1): {
        1: ((Links.first, 8),),
        3: ((Links.second, 7),),
        7: ((Links.second, 8),),
    },
    (OUTPUT, 1): {
        None: ((Links.ready, 6),),
    },
    (FEED, 1): {
        None: ((Links.third, 7), (Links.ready, 7),),
    },
    (GELU, 1): {
        0: ((Links.ready, 8),),
    },
    (BACK_TILE, 1): {
        3: ((E0, 1, 1),),
        5: ((E0, 2, 1),),
    },
    (BACK_FEED, 1): {
        None: ((E1, 1, 1),),
    },
    (BACK_OUTPUT, 1): {
        None: ((O, 1, 1), (R0, 2, 1), (R1, 2, 1),),
    },
    (BACK_HEAD, 1): {
        0: ((E0, 3, 1), (E1, 2, 1), (O, 2, 1),),
        2: ((R0, 3, 1), (M0, 2, 1),),
        3: ((R1, 3, 1),),
        4: ((E0, 4, 1), (M1, 2, 1),),
        6: ((O, 3, 1), (M2, 2, 1),),
        7: ((E0, 5, 1), (R0, 4, 1), (M0, 3, 1),),
    },
    (BACK_PAIR, 1): {
        0: ((M0, 1, 1),),
        1: ((M1, 1, 1),),
        2: ((M2, 1, 1), (E1, 3, 1),),
        3: ((M3, 1, 1),),
    },
    (BACK_MIXER, 1): {
        None: ((R1, 4, 1), (M3, 2, 1),),
    },
    (BACK_LAYER, 1): {
        None: ((M1, 3, 1),),
    },
    (BACK_TILE, 0): {
        0: ((E0, 6, 1), (R0, 5, 1), (E1, 4, 1), (O, 4, 1), (M2, 3, 1),),
        1: ((M0, 4, 1), (M3, 3, 1), (R1, 5, 1), (M1, 4, 1),),
        2: ((M2, 4, 1),),
        3: ((E0, 1, 0), (R0, 6, 1), (E1, 5, 1), (E0, 7, 1), (M3, 4, 1),),
        4: ((O, 5, 1),),
        5: ((R1, 6, 1), (M0, 5, 1), (M1, 5, 1), (E0, 2, 0),),
        6: ((M2, 5, 1), (E1, 6, 1), (M3, 5, 1),),
        7: ((O, 6, 1), (R0, 7, 1),),
    },
    (BACK_FEED, 0): {
        None: ((E1, 1, 0),),
    },
    (BACK_OUTPUT, 0): {
        None: ((O, 1, 0), (M0, 6, 1), (R0, 2, 0), (M1, 6, 1),),
    },
    (BACK_HEAD, 0): {
        0: ((M2, 6, 1), (M3, 6, 1), (R1, 7, 1), (E0, 3, 0), (R1, 2, 0),),
        1: ((E1, 7, 1), (E1, 2, 0),),
        2: ((M0, 7, 1), (O, 7, 1), (R0, 3, 0), (E0, 4, 0), (M0, 2, 0), (O, 2, 0),),
        3: ((M1, 7, 1), (M2, 7, 1),),
        4: ((M3, 7, 1), (R1, 3, 0), (E0, 5, 0), (M1, 2, 0),),
        5: ((E1, 3, 0),),
        6: ((R0, 4, 0), (M2, 2, 0), (M0, 3, 0),),
        7: ((E0, 6, 0), (O, 3, 0),),
    },
    (BACK_PAIR, 0): {
        0: ((M0, 1, 0),),
        1: ((M1, 1, 0),),
        2: ((M2, 1, 0),),
        3: ((M3, 1, 0),),
    },
    (BACK_MIXER, 0): {
        None: ((R0, 5, 0), (R1, 4, 0), (M3, 2, 0), (M1, 3, 0),),
    },
    (END, 0): {
        None: (
            (T, 1, 0), (E1, 4, 0), (M2, 3, 0), (T, 2, 0), (M0, 4, 0), (R1, 5, 0), (O, 4, 0), (M3, 3, 0), (R0, 6, 0), (M1, 4, 0),
            (M2, 4, 0), (E1, 5, 0), (T, 3, 0), (M0, 5, 0), (M3, 4, 0), (O, 5, 0), (R1, 6, 0), (T, 4, 0), (M1, 5, 0), (M2, 5, 0),
            (E1, 6, 0), (M3, 5, 0), (M0, 6, 0), (T, 5, 0), (O, 6, 0), (M1, 6, 0), (M2, 6, 0), (M3, 6, 0), (T, 6, 0), (E0, 7, 0),
            (R0, 7, 0), (R1, 7, 0), (E1, 7, 0), (M0, 7, 0), (O, 7, 0), (M1, 7, 0), (M2, 7, 0), (M3, 7, 0), (T, 7, 0),
        ),
    },
}

PLAIN_IN = ("columns", "table", "gm", "gf", "gz", "wm", "wo", "we", "wr")
PLAIN_OUT = ("loss", "lg", "kept_m", "kept_near", "dtable", "dgm", "dgf", "dgz", "dwm", "dwo", "dwe", "dwrt")
LINKED_IN = ("tokens", "mask", "emb", "mgain", "fgain", "zgain", "wm_s", "wo_s", "we_s", "wr_s")
LINKED_OUT = ("loss", "lg", "kept_m", "kept_near", "out_m", "out_o", "out_e", "out_r", "out_t")
SCRATCH = dict(
    x=pltpu.VMEM((LAYERS, LEN, D), F32),
    x1=pltpu.VMEM((LAYERS, LEN, D), F32),
    dx=pltpu.VMEM((LEN, D), F32),
    kv=pltpu.VMEM((LAYERS, LEN, 2 * D), BF16),
    pT=pltpu.VMEM((LAYERS, 3 * D, LEN), BF16),
    inv1s=pltpu.VMEM((LAYERS, HEADS, 1, LEN), F32),
    cum=pltpu.VMEM((LAYERS, D, LEN), F32),
    oT=pltpu.VMEM((LAYERS, D, LEN), BF16),
    hT=pltpu.VMEM((LAYERS, D, LEN), BF16),
    g=pltpu.VMEM((LEN, D), BF16),
    gT=pltpu.VMEM((LAYERS, D, LEN), BF16),
    wide=pltpu.VMEM((LEN, LEN), BF16),
    a1k=pltpu.VMEM((D, LEN), BF16),
    m=pltpu.VMEM((2, LEN, LEN), BF16),
    near=pltpu.VMEM((2, CHUNKS, CH + REACH, CH), F32),
    keep_sem=pltpu.SemaphoreType.DMA((2, 2)),
    d=pltpu.VMEM((LEN, LEN), BF16),
    ds=pltpu.VMEM((LEN, 2 * CH), BF16),
    doT=pltpu.VMEM((D, LEN), BF16),
    dpT=pltpu.VMEM((3 * D, LEN), BF16),
    yb=pltpu.VMEM((LEN, D), BF16),
    acc=pltpu.VMEM((LEN, D), F32),
)
PLAIN_SCRATCH = dict(
    stage=pltpu.VMEM((4, D, TILE), BF16),
    stage_half=pltpu.VMEM((4, D, BACK), BF16),
    sem=pltpu.SemaphoreType.DMA((4,)),
    sem_half=pltpu.SemaphoreType.DMA((4,)),
)


def sum_buffers(n, rows, cols, along):
    def shape(blocks):
        return (rows * blocks // 8, cols) if along == 0 else (rows, cols * blocks // 8)

    return {
        "grad_" + n: pltpu.VMEM((rows, cols), BF16),
        "r1" + n: pltpu.VMEM(shape(4), BF16),
        "r2" + n: pltpu.VMEM(shape(2), BF16),
        "r3" + n: pltpu.VMEM(shape(1), BF16),
        "rz" + n: pltpu.VMEM((2,) + shape(1), BF16),
    }


LINKED_SCRATCH = dict(
    table=pltpu.VMEM((D, 384), BF16),
    wm=pltpu.VMEM((LAYERS, D, 3 * D), BF16),
    wo=pltpu.VMEM((LAYERS, D, D), BF16),
    we=pltpu.VMEM((LAYERS, D, FF), BF16),
    wr=pltpu.VMEM((LAYERS, FF, D), BF16),
    columns=pltpu.VMEM((LEN, 8), jnp.int32),
    tz=pltpu.VMEM((4, 64, 128), BF16),
    gains=pltpu.VMEM((8, D), F32),
    lgs=pltpu.VMEM((4, 64, LEN), BF16),
    losss=pltpu.VMEM((8, 128), F32),
    send_sem=pltpu.SemaphoreType.DMA((9, 15)),
    recv_sem=pltpu.SemaphoreType.DMA((9, 15)),
    zsend=pltpu.SemaphoreType.DMA((3, 4)),
    zrecv=pltpu.SemaphoreType.DMA((3, 4)),
    load_sem=pltpu.SemaphoreType.DMA((LAYERS, 9)),
    sum_send=pltpu.SemaphoreType.DMA((10, 10)),
    sum_recv=pltpu.SemaphoreType.DMA((10, 9)),
    tile_send=pltpu.SemaphoreType.DMA((4,)),
    tile_recv=pltpu.SemaphoreType.DMA((4,)),
    dtable=pltpu.VMEM((D, VOCAB), F32),
    dgains=pltpu.VMEM((8, D), F32),
    **sum_buffers("m", D, 3 * D, 0),
    **sum_buffers("o", D, D, 0),
    **sum_buffers("e", D, FF, 0),
    **sum_buffers("r", D, FF, 1),
    **sum_buffers("t", D, 384, 0),
)


def local_step(linked, *operands):
    vmem = pl.BlockSpec(memory_space=pltpu.VMEM)
    hbm = pl.BlockSpec(memory_space=pl.ANY)
    shape = jax.ShapeDtypeStruct
    kept = (shape((LAYERS, HEADS, LEN, LEN), BF16), shape((LAYERS, HEADS, CHUNKS, CH + REACH, CH), F32))
    if linked:
        scratch = dict(SCRATCH, **LINKED_SCRATCH)
        in_specs = [vmem] * 6 + [hbm] * 4
        out_shape = (
            shape((4, 8, 128), F32),
            shape((4, 64, LEN), BF16),
            *kept,
            shape((LAYERS, 4, 64, 384), BF16),
            shape((LAYERS, 64, D), BF16),
            shape((LAYERS, 64, FF), BF16),
            shape((LAYERS, D, 256), BF16),
            shape((64, 384), BF16),
        )
        out_specs = (hbm,) * 9
    else:
        scratch = dict(SCRATCH, **PLAIN_SCRATCH)
        in_specs = [vmem] * len(operands)
        out_shape = (
            shape((8, 128), F32),
            shape((LEN, VOCAB), BF16),
            *kept,
            shape((D, VOCAB), F32),
            shape((LAYERS, 1, D), F32),
            shape((LAYERS, 1, D), F32),
            shape((1, D), F32),
            shape((LAYERS, D, 3 * D), BF16),
            shape((LAYERS, D, D), BF16),
            shape((LAYERS, D, FF), BF16),
            shape((LAYERS, D, FF), BF16),
        )
        out_specs = (vmem,) * 2 + (hbm,) * 2 + (vmem,) * 4 + (hbm,) * 4
    return pl.pallas_call(
        functools.partial(step_kernel, linked),
        out_shape=out_shape,
        in_specs=in_specs,
        out_specs=out_specs,
        scratch_shapes=list(scratch.values()),
        compiler_params=pltpu.CompilerParams(
            vmem_limit_bytes=64 * 1024 * 1024,
            collective_id=0 if linked else None,
            has_side_effects=linked,
        ),
        cost_estimate=pl.CostEstimate(flops=40_000_000_000, bytes_accessed=40_000_000, transcendentals=0),
        name="local_step",
    )(*operands)


def finish_kernel(
    loss_in, lg_in, dwm_in, dwo_in, dwe_in, dwrt_in, last_in,
    out_loss, out_lg, out_table, out_m, out_o, out_mgain, out_e, out_r, out_fgain, out_zgain,
    loss, lg, dwm, dwo, dwe, dwrt, last, sem,
):
    pairs = ((loss_in, loss), (lg_in, lg), (dwm_in, dwm), (dwo_in, dwo), (dwe_in, dwe), (dwrt_in, dwrt), (last_in, last))
    copies = [pltpu.make_async_copy(src, dst, sem.at[i]) for i, (src, dst) in enumerate(pairs)]
    every(copies, START)
    every(copies, WAIT)
    z = lax.axis_index(SECTION)
    r, c = iotas(4, 128)
    out_loss[...] = jnp.sum(jnp.where(r == c, loss[:, 0, :], 0.0), axis=0, keepdims=True)
    out_lg[...] = lg[...].astype(F32)
    table = last[:, :VOCAB].astype(F32)
    out_table[...] = sum(jnp.where(z == i, table[:, 64 * i:64 * (i + 1)], 0.0) for i in range(4))
    gains = last[:, VOCAB:].astype(F32)
    gains = jnp.concatenate([gains, jnp.zeros((64, 128), F32)], axis=0).T
    out_mgain[...] = gains[0:2, :64]
    out_fgain[...] = gains[2:4, :64]
    out_zgain[...] = gains[4:5, :64]
    out_o[...] = dwo[...].astype(F32)
    out_e[...] = dwe[...].astype(F32)
    for l in range(LAYERS):
        out_r[l] = dwrt[l].astype(F32).T
        for p in range(4):
            for j in range(3):
                out_m[l, :, D * j + CH * p:D * j + CH * (p + 1)] = dwm[l, p, :, CH * j:CH * (j + 1)].astype(F32)


def finish(*operands):
    vmem = pl.BlockSpec(memory_space=pltpu.VMEM)
    shapes = (
        (1, 128), (4, 64, LEN), (64, 64), (LAYERS, 64, 3 * D), (LAYERS, 64, D), (LAYERS, 64), (LAYERS, 64, FF),
        (LAYERS, 256, D), (LAYERS, 64), (1, 64),
    )
    return pl.pallas_call(
        finish_kernel,
        out_shape=tuple(jax.ShapeDtypeStruct(shape, F32) for shape in shapes),
        in_specs=[pl.BlockSpec(memory_space=pl.ANY)] * len(operands),
        out_specs=(vmem,) * len(shapes),
        scratch_shapes=[pltpu.VMEM(operand.shape, operand.dtype) for operand in operands]
        + [pltpu.SemaphoreType.DMA((len(operands),))],
        compiler_params=pltpu.CompilerParams(vmem_limit_bytes=60 * 1024 * 1024),
        name="finish",
    )(*operands)


def body(
    tokens,
    padding_mask,
    embedding,
    mixer_weight,
    output_weight,
    mixer_gain,
    expand_weight,
    reduce_weight,
    feed_gain,
    final_gain,
):
    segments = lax.axis_size(SECTION)
    segment_index = lax.axis_index(SECTION)
    item_count = tokens.shape[0]
    assert item_count == segments
    slice_width = embedding.shape[1]

    if segments == 4 and lax.axis_size(DP) == 8:
        loss, lg, _, _, dwm, dwo, dwe, dwrt, last = local_step(
            True, tokens, padding_mask, embedding, mixer_gain, feed_gain, final_gain[None],
            mixer_weight, output_weight, expand_weight, reduce_weight,
        )
        loss, lg, table_grad, dwm, dwo, mixer_gain_grad, dwe, dwr, feed_gain_grad, final_gain_grad = finish(
            loss, lg, dwm, dwo, dwe, dwrt, last
        )
        return (
            loss[0, :4], jnp.swapaxes(lg, 1, 2), table_grad, dwm, dwo, mixer_gain_grad, dwe, dwr, feed_gain_grad, final_gain_grad[0]
        )

    token_row = lax.dynamic_index_in_dim(tokens, segment_index, 0, keepdims=False)
    mask_row = lax.dynamic_index_in_dim(padding_mask, segment_index, 0, keepdims=False)
    zero = jnp.zeros((1,), jnp.int32)
    columns = jnp.stack(
        [token_row, jnp.concatenate([token_row[1:], zero]), jnp.concatenate([mask_row[1:], zero])], axis=1
    )

    def gather(block, dim):
        return lax.all_gather(block.astype(BF16), DP, axis=dim, tiled=True)

    table = lax.all_gather(gather(embedding, 0), SECTION, axis=1, tiled=True)
    gains = gather(jnp.concatenate([mixer_gain, feed_gain, final_gain[None]], axis=0), 1).astype(F32)
    loss, lg, _, _, dtable, dgm, dgf, dgz, dwm, dwo, dwe, dwrt = local_step(
        False, columns, table, gains[0:2, None], gains[2:4, None], gains[4:5],
        gather(mixer_weight, 1), gather(output_weight, 1), gather(expand_weight, 1), gather(reduce_weight, 1),
    )
    item_loss = lax.all_gather(loss[0, 0], SECTION)
    parts = lg.reshape(LEN, segments, slice_width).transpose(1, 0, 2)
    logit_grad = lax.all_to_all(parts, SECTION, 0, 0, tiled=True).astype(F32)

    def shard(grad, dim):
        part = lax.psum_scatter(grad.astype(BF16), DP, scatter_dimension=dim, tiled=True)
        return lax.psum(part, SECTION).astype(F32)

    table_part = lax.psum_scatter(dtable.astype(BF16), DP, scatter_dimension=0, tiled=True)
    table_grad = lax.psum_scatter(table_part, SECTION, scatter_dimension=1, tiled=True).astype(F32)
    gain_grads = lax.psum_scatter(
        jnp.concatenate([dgm[:, 0], dgf[:, 0], dgz], axis=0), DP, scatter_dimension=1, tiled=True
    )
    gain_grads = lax.psum(gain_grads, SECTION)
    return (
        item_loss,
        logit_grad,
        table_grad,
        shard(dwm, 1),
        shard(dwo, 1),
        gain_grads[0:2],
        shard(dwe, 1),
        jnp.swapaxes(shard(dwrt, 2), 1, 2),
        gain_grads[2:4],
        gain_grads[4],
    )


def solution(mesh):
    placed = (
        P(DP, None),
        P(DP, None),
        P(DP, SECTION),
        P(None, DP, None),
        P(None, DP, None),
        P(None, DP),
        P(None, DP, None),
        P(None, DP, None),
        P(None, DP),
        P(DP),
    )
    return jax.shard_map(
        body,
        mesh=mesh,
        in_specs=placed,
        out_specs=(
            P(DP),
            P(DP, None, SECTION),
            P(DP, SECTION),
            P(None, DP, None),
            P(None, DP, None),
            P(None, DP),
            P(None, DP, None),
            P(None, DP, None),
            P(None, DP),
            P(DP),
        ),
        check_vma=False,
    )
```

profile of v0, /device:TPU:0, one launch (start us, length us, event | category | flops | bytes accessed | tf_op | source)
XLA Modules:
  0.0 189.9 jit_solution(9137208246133647929)
XLA Ops:
  0.6 184.5 %local_step.1 = (f32[4,8,128]{2,1,0:T(8,128)}, bf16[4,64,640]{2,1,0:T(8,128)(2,1)}, bf16[2,8,640,640]{3,2,1,0:T(8,128)(2,1)}, f32[2,8,5,160,128]{4,3,2,1,0:T(8,1...) custom-call(s32[4,640]{1,0:T(4,128)} %refs_0_.1, ...), custom_call_target="tpu_custom_call" | custom-call | flops 40000000000 | bytes 40000000 | tf_op jit(solution)/shard_map/local_step/pallas_call | solution.py:1150
  185.1 3.7 %finish.1 = (f32[1,128]{1,0:T(1,128)}, f32[4,64,640]{2,1,0:T(8,128)}, f32[64,64]{1,0:T(8,128)}, f32[2,64,1536]{2,1,0:T(8,128)}, f32[2,64,512]{2,1,0:T(8,128)}, /...) custom-call(f32[4,8,128]{2,1,0:T(8,128)} %get-tuple-element.27.loss_, ...), custom_call_target="tpu_custom_call" | custom-call | tf_op jit(solution)/shard_map/finish/pallas_call | solution.py:1201
  188.8 1.1 slice_bitcast_fusion
where the time goes:
time: 190 us
  Pallas kernels  188 us (99%)
    pallas_call x1, Pallas kernels, local_step(): pl.pallas_call(functools.partial(step_kernel, linked), out_shape=out_shap...  184 us

commit v1 on v0

--- a/solution.py
+++ b/solution.py
@@ -256,7 +256,7 @@
             device_id={DP: self.links.core_n}, device_id_type=pl.DeviceIdType.MESH,
         )
 
-    def copy(self, name, kind, l=None):
+    def copy(self, name, kind, l=0):
         piece = self.pieces[name]
         core, x, y, z, links = self.core, self.x, self.y, self.z, self.links
         mine = 4 * core
@@ -271,11 +271,11 @@
         elif kind == 3:
             src, dst = pair(mine + 2 * (1 - y), piece.r2, 0, 2, 1)
         elif kind == 4:
-            src, dst = pair(mine + 2 * (1 - y) + x, piece.r3, 0, 1, 0)
+            src, dst = pair(mine + 2 * (1 - y) + x, piece.r3[l], 0, 1, 0)
         elif kind == 5:
-            src, dst = pair(mine + 2 * y + 1 - x, piece.r3, 0, 1, 1)
+            src, dst = pair(mine + 2 * y + 1 - x, piece.r3[l], 0, 1, 1)
         else:
-            src = piece.r3
+            src = piece.r3[l]
             dst = piece.rz.at[kind - 6] if kind < 8 else piece.out(l)
         device = (
             {DP: links.core_n}, {DP: links.x_n}, {DP: links.x_n}, {DP: links.y_n}, {DP: links.y_n}, {DP: links.x_n},
@@ -286,62 +286,100 @@
             device_id=device, device_id_type=pl.DeviceIdType.MESH,
         )
 
+    def tile_parts(self, block):
+        y, x = block // 2, block % 2
+        copies = []
+        for name in (R0, R1):
+            piece = self.pieces[name]
+            for half, kind, to, at in ((0, 1 + y, {DP: self.links.x_n}, y), (1, 3 + 7 * x, {DP: self.links.y_n}, x)):
+                copies.append(pltpu.make_async_remote_copy(
+                    src_ref=self.view(piece, piece.grad, 4 * self.core + block, 1, half), dst_ref=self.view(piece, piece.r2, at, 1, half),
+                    send_sem=self.send_sem.at[piece.index, kind], recv_sem=self.recv_sem.at[piece.index, kind],
+                    device_id=to, device_id_type=pl.DeviceIdType.MESH,
+                ))
+        return copies
+
+    def tile_step(self, block):
+        self.tile_copy(block).wait_recv()
+        r = self.pieces[R0]
+        mine = pl.ds(pl.multiple_of((4 * self.core + block) * r.size, r.size), r.size)
+        self.add(r.whole.at[:, mine], r.whole_r1.at[:, r.size * block:r.size * (block + 1)])
+        first0, second0, first1, second1 = self.tile_parts(block)
+
+        @pl.when(self.x != block % 2)
+        def _():
+            first0.start()
+            first1.start()
+
+        @pl.when(self.y != block // 2)
+        def _():
+            second0.start()
+            second1.start()
+
     def add(self, into, other):
         into[...] = (into[...].astype(F32) + other[...].astype(F32)).astype(BF16)
 
     def step(self, name, number, l):
         piece = self.pieces[name]
-        grad, r1, r2, r3, rz = piece.grad, piece.r1, piece.r2, piece.r3, piece.rz
+        grad, r1, r2, r3, rz = piece.grad, piece.r1, piece.r2, piece.r3[l], piece.rz
         mine = 4 * self.core
         own = mine + 2 * self.y + self.x
         tiles = name in (R0, R1)
         if number == 1:
-            self.copy(name, 0).start()
+            self.copy(name, 0, l).start()
+        elif number == 2 and tiles:
+            if name == R0:
+                self.tile_step(3)
         elif number == 2:
-            if not tiles:
-                self.copy(name, 0).wait_recv()
-            elif name == R0:
-                for block in range(4):
-                    self.tile_copy(block).wait_recv()
+            self.copy(name, 0, l).wait_recv()
             self.add(self.view(piece, grad, mine, 4), self.view(piece, r1, 0, 4))
             for kind in (1, 2, 3):
-                self.copy(name, kind).start()
+                self.copy(name, kind, l).start()
         elif number == 3:
             for kind in (1, 2):
-                self.copy(name, kind).wait_recv()
+                self.copy(name, kind, l).wait_recv()
                 self.add(self.view(piece, grad, mine + 2 * (kind - 1) + self.x, 1, 0), self.view(piece, r2, kind - 1, 1, 0))
-            self.copy(name, 3).wait_recv()
-            self.copy(name, 4).start()
+            if tiles:
+                for i in range(2):
+                    self.half_block(name, i).wait_recv()
+            else:
+                self.copy(name, 3, l).wait_recv()
             self.add(self.view(piece, grad, mine + 2 * self.y, 2, 1), self.view(piece, r2, 0, 2, 1))
-            self.copy(name, 5).start()
+            self.copy(name, 4, l).start()
+            self.copy(name, 5, l).start()
         elif number == 4:
             for half in (0, 1):
-                self.copy(name, 4 + half).wait_recv()
+                self.copy(name, 4 + half, l).wait_recv()
                 self.add(self.view(piece, r3, 0, 1, half), self.view(piece, grad, own, 1, half))
 
             @pl.when(self.outer)
             def _():
-                self.copy(name, 6).start()
+                self.copy(name, 6, l).start()
 
             if not tiles:
-                self.copy(name, 0).wait_send()
+                self.copy(name, 0, l).wait_send()
             elif name == R0:
                 for block in range(4):
                     self.tile_copy(block).wait_send()
-            for kind in range(1, 6):
-                self.copy(name, kind).wait_send()
+            for kind in (1, 2, 4, 5):
+                self.copy(name, kind, l).wait_send()
+            if tiles:
+                for i in range(2):
+                    self.half_block(name, i).wait_send()
+            else:
+                self.copy(name, 3, l).wait_send()
         elif number == 5:
 
             @pl.when(self.inner)
             def _():
-                self.copy(name, 6).wait_recv()
+                self.copy(name, 6, l).wait_recv()
                 self.add(r3, rz.at[0])
-                self.copy(name, 7).start()
+                self.copy(name, 7, l).start()
         elif number == 6:
 
             @pl.when(self.inner)
             def _():
-                self.copy(name, 7).wait()
+                self.copy(name, 7, l).wait()
                 self.add(r3, rz.at[1])
                 self.copy(name, 8, l).start()
                 self.local(piece, l).start()
@@ -349,7 +387,7 @@
 
             @pl.when(self.outer)
             def _():
-                self.copy(name, 6).wait_send()
+                self.copy(name, 6, l).wait_send()
                 self.copy(name, 8, l).wait_recv()
 
             @pl.when(self.inner)
@@ -357,8 +395,17 @@
                 self.copy(name, 8, l).wait_send()
                 self.local(piece, l).wait()
 
+    def half_block(self, name, x):
+        piece = self.pieces[name]
+        view = self.view(piece, piece.r2, x, 1, 1)
+        return pltpu.make_async_remote_copy(
+            src_ref=view, dst_ref=view,
+            send_sem=self.send_sem.at[piece.index, 3 + 7 * x], recv_sem=self.recv_sem.at[piece.index, 3 + 7 * x],
+            device_id={DP: self.links.y_n}, device_id_type=pl.DeviceIdType.MESH,
+        )
+
     def local(self, piece, l):
-        return pltpu.make_async_copy(piece.r3, piece.out(l), self.send_sem.at[piece.index, 9])
+        return pltpu.make_async_copy(piece.r3[l], piece.out(l), self.send_sem.at[piece.index, 9])
 
 
 class Piece:
@@ -370,7 +417,9 @@
 
 def sum_pieces(refs, out_m, out_o, out_e, out_r, out_t):
     def part(n, index):
-        return [refs[name + n].at[index] for name in ("grad_", "r1", "r2", "r3")] + [refs["rz" + n].at[(slice(None),) + index]]
+        views = [refs[name + n].at[index] for name in ("grad_", "r1", "r2")]
+        views.append([refs["r3" + n].at[(l,) + index] for l in range(1 if n == "t" else LAYERS)])
+        return views + [refs["rz" + n].at[(slice(None),) + index]]
 
     every = slice(None)
     pieces = {}
@@ -405,7 +454,7 @@
 
 
 def step_body(
-    linked, loss, lg, kept_m, kept_near, x, x1, dx, kv, pT, inv1s, cum, oT, hT, g, gT, wide, a1k, m, near, keep_sem, d, ds, doT, dpT, yb, acc,
+    linked, loss, lg, kept_m, kept_near, x, x1, dx, keys, values, pT, inv1s, cum, oT, hT, g, gT, wide, a1k, m, near, keep_sem, d, ds, doT, dpT, yb, acc,
     columns=None, table=None, gm=None, gf=None, gz=None, wm=None, wo=None, we=None, wr=None, stage=None, stage_half=None, sem=None, sem_half=None,
     dtable=None, dgm=None, dgf=None, dgz=None, dwm=None, dwo=None, dwe=None, dwrt=None,
     tokens=None, mask=None, emb=None, mgain=None, fgain=None, zgain=None, wm_s=None, wo_s=None, we_s=None, wr_s=None, tz=None, gains=None, lgs=None, losss=None,
@@ -417,12 +466,12 @@
     wm_ref, wo_ref, we_ref, wr_ref = wm, wo, we, wr
     loss_ref, lg_ref, dtable_ref, dgm_ref, dgf_ref, dgz_ref = loss, lg, dtable, dgm, dgf, dgz
     dwm_ref, dwo_ref, dwe_ref, dwrt_ref = dwm, dwo, dwe, dwrt
-    x_ref, x1_ref, dx_ref, kv_ref, pT_ref, inv1_ref, cum_ref = x, x1, dx, kv, pT, inv1s, cum
+    x_ref, x1_ref, dx_ref, pT_ref, inv1_ref, cum_ref = x, x1, dx, pT, inv1s, cum
     oT_ref, hT_ref, g_ref, gT_ref, wide_ref, a1k_ref, near_ref, m_ref, d_ref, ds_ref = oT, hT, g, gT, wide, a1k, near, m, d, ds
     doT_ref, dpT_ref, w_ref, yb_ref, acc_ref = doT, dpT, a1k, yb, acc
     xs = [x_ref.at[0], x_ref.at[1], dx_ref]
     placed = by_position if linked else (lambda rows: rows)
-    r, c = iotas(LEN, LEN)
+    r, c = iotas(2 * CH, 2 * CH)
     upper = (r <= c).astype(F32).astype(BF16)
 
     if linked:
@@ -546,6 +595,8 @@
                 for act in acts:
                     if isinstance(act[0], int):
                         sums.step(*act)
+                    elif act[0] is Sums.tile_step:
+                        sums.tile_step(act[1])
                     else:
                         act[0](links, *act[1:])
 
@@ -556,8 +607,8 @@
 
     inv2 = 1.0 / (lax.broadcasted_iota(jnp.int32, (1, LEN), 1).astype(F32) + 1.0)
 
-    def emit(slot, wait_first, value, dst):
-        into, sems = (stage, sem) if dst.shape[1] == TILE else (stage_half, sem_half)
+    def emit(slot, wait_first, value, dst, pool=0):
+        into, sems = (stage, sem) if pool == 0 else (stage_half, sem_half)
 
         def copy():
             return pltpu.make_async_copy(into.at[slot], dst, sems.at[slot])
@@ -580,10 +631,9 @@
             dgz_ref[...] = value
 
     def by_rows(run, init=None):
-        def some(i, carry):
-            return run(pl.ds(pl.multiple_of(i * CH, CH), CH), carry)
-
-        return lax.fori_loop(0, CHUNKS, some, init)
+        for i in range(CHUNKS):
+            init = run(slice(i * CH, (i + 1) * CH), init)
+        return init
 
     def normed_rows(src, gain, dst, dstT):
         def some(rows, carry):
@@ -623,20 +673,24 @@
     m_ref[...] = jnp.zeros_like(m_ref)
     near_ref[...] = jnp.zeros_like(near_ref)
 
+    def key_sums(l):
+        a1k_ref[...] = feature_parts(pT_ref[l, D:2 * D, :].astype(F32))[0].astype(BF16)
+        for t0, t1 in WIDE:
+            total = mm(a1k_ref[:, t0:t1], wide_ref[:t1 - t0, :t1 - t0])
+            cum_ref[:, t0:t1] = total if t0 == 0 else total + cum_ref[:, t0 - 1:t0]
+
     def attention_forward(l):
         normed_rows(x_ref.at[l], gm_ref[l], yb_ref, hT_ref.at[l])
         h = yb_ref[...]
         for j in range(3):
             part = mm(h, wm_ref[l, :, j * TILE:(j + 1) * TILE]).astype(BF16)
-            if j > 0:
-                kv_ref[l, :, (j - 1) * TILE:j * TILE] = part
+            if j == 1:
+                keys[...] = part
+            if j == 2:
+                values[l] = part
             pT_ref[l, j * TILE:(j + 1) * TILE, :] = part.T
         service((MIXER, l))
-        kT = pT_ref[l, D:2 * D, :].astype(F32)
-        a1k_ref[...] = feature_parts(kT)[0].astype(BF16)
-        for i in range(CHUNKS):
-            t0, t1 = i * CH, (i + 1) * CH
-            cum_ref[l, :, t0:t1] = mm(a1k_ref[:, :t1], wide_ref[:t1, t0:t1])
+        key_sums(l)
 
         def pair(p, carry):
             base = pl.multiple_of(p * CH, CH)
@@ -653,12 +707,12 @@
                 first_k, _, second_k = feature_parts(kT.astype(F32))
                 key_feat = jnp.concatenate([first_k.astype(BF16), second_k.astype(BF16)], axis=0).T
                 first_q = feature_parts(qT.astype(F32))[0].astype(BF16).astype(F32)
-                total = jnp.sum(first_q * cum_ref[l, pl.ds(row, HD), :], axis=0, keepdims=True)
+                total = jnp.sum(first_q * cum_ref[pl.ds(row, HD), :], axis=0, keepdims=True)
                 inv1 = 1.0 / (total + 1.0)
                 inv1_ref[l, 2 * p + e] = inv1
                 query_feat2 = query_features(qT, inv1, inv2)[3]
                 key_feat2 = jnp.concatenate([key_feat, key_feat], axis=1)
-                key_nat = kv_ref[l, :, pl.ds(base, CH)]
+                key_nat = keys[:, pl.ds(base, CH)]
                 query_masked = masked_pair(qT, e)
                 for t0, t1 in WIDE:
                     mixture = mixture_block(t0, t1, key_nat, key_feat2, query_masked, query_feat2, near_ref.at[e])
@@ -680,14 +734,14 @@
         service((FEED, l))
 
         def tile(j, carry):
-            col = pl.multiple_of(j * BACK, BACK)
-            active = gelu_parts(mm(g_ref[...], we_ref[l, :, pl.ds(col, BACK)]))[0].astype(BF16)
+            col = pl.multiple_of(j * TILE, TILE)
+            active = gelu_parts(mm(g_ref[...], we_ref[l, :, pl.ds(col, TILE)]))[0].astype(BF16)
             service((GELU, l), j)
-            xs[l + 1][...] += mm(active, wr_ref[l, pl.ds(col, BACK), :])
+            xs[l + 1][...] += mm(active, wr_ref[l, pl.ds(col, TILE), :])
             service((FEED_TILE, l), j)
             return carry
 
-        lax.fori_loop(0, FF // BACK, tile, 0)
+        lax.fori_loop(0, FF // TILE, tile, 0)
 
     def head():
         zT_ref, grad_ref = doT_ref, yb_ref.at[:, :VOCAB]
@@ -736,7 +790,11 @@
             pltpu.make_async_copy(losss, loss_ref.at[zi], zsend.at[2, 3]).start()
         else:
             loss_ref[...] = loss
-        dtable_ref[...] = mm(zT_ref[...], grad_ref[...])
+        dtable_head = mm(zT_ref[...], grad_ref[...])
+        if linked:
+            sums_refs["grad_t"][:, :VOCAB] = dtable_head.astype(BF16)
+        else:
+            dtable_ref[...] = dtable_head
 
     def feed_backward(l):
         def some(rows, carry):
@@ -751,35 +809,38 @@
         acc_ref[...] = jnp.zeros_like(acc_ref)
 
         def tile(j, carry):
-            col = pl.multiple_of(j * BACK, BACK)
+            col = pl.multiple_of(j * TILE, TILE)
             slot = lax.rem(j, 2)
             later = (j >= 2) if l == LAYERS - 1 else True
-            value, slope = gelu_parts(mm(g_ref[...], we_ref[l, :, pl.ds(col, BACK)]))
+            value, slope = gelu_parts(mm(g_ref[...], we_ref[l, :, pl.ds(col, TILE)]))
             dreduce = mm(doT_ref[...], value.astype(BF16))
             if linked:
-                place = pl.multiple_of(BACK * (lax.rem(j, 2) * 4 + lax.div(j, 2)), BACK)
-                sums_refs["grad_r"][:, pl.ds(place, BACK)] = dreduce.astype(BF16)
-                pl.when(lax.rem(j, 2) != sums.core)(lambda: sums.tile_copy(lax.div(j, 2)).start())
+                for i in range(2):
+                    place = pl.multiple_of(BACK * j + FF // 2 * i, BACK)
+                    sums_refs["grad_r"][:, pl.ds(place, BACK)] = dreduce[:, BACK * i:BACK * (i + 1)].astype(BF16)
+                sums.tile_copy(j).start()
             else:
-                emit(slot, later, dreduce, dwrt_ref.at[l, :, pl.ds(col, BACK)])
-            dact = mm_nt(yb_ref[...], wr_ref[l, pl.ds(col, BACK), :])
+                emit(slot, later, dreduce, dwrt_ref.at[l, :, pl.ds(col, TILE)], 1)
+            dact = mm_nt(yb_ref[...], wr_ref[l, pl.ds(col, TILE), :])
             dhid = (dact * slope).astype(BF16)
             dexpand = mm(gT_ref[l], dhid)
             if linked:
-                sums_refs["grad_e"][:, pl.ds(col, BACK)] = dexpand.astype(BF16)
+                sums_refs["grad_e"][:, pl.ds(col, TILE)] = dexpand.astype(BF16)
             else:
-                emit(2 + slot, later, dexpand, dwe_ref.at[l, :, pl.ds(col, BACK)])
-            dnormed = mm_nt(dhid, we_ref[l, :, pl.ds(col, BACK)])
+                emit(2 + slot, later, dexpand, dwe_ref.at[l, :, pl.ds(col, TILE)], 1)
+            dnormed = mm_nt(dhid, we_ref[l, :, pl.ds(col, TILE)])
 
             acc_ref[...] += dnormed
             service((BACK_TILE, l), j)
             return carry
 
-        lax.fori_loop(0, FF // BACK, tile, 0)
+        lax.fori_loop(0, FF // TILE, tile, 0)
         service((BACK_FEED, l))
         back_rows(x1_ref.at[l], gf_ref[l], 2 + l)
 
     def attention_backward(l):
+        if l < LAYERS - 1:
+            key_sums(l)
         yb_ref[...] = dx_ref[...].astype(BF16)
         yb = yb_ref[...]
         doutput = mm(placed(oT_ref[l]), yb)
@@ -805,7 +866,7 @@
                 first_q, slope1_q, second_q, query_feat2 = query_features(qT, inv1, inv2)
                 first_k, slope1_k, second_k = feature_parts(kT.astype(F32))
                 key_featT = jnp.concatenate([first_k.astype(BF16), second_k.astype(BF16)], axis=0)
-                value_nat = kv_ref[l, :, pl.ds(pl.multiple_of(D + base, CH), CH)]
+                value_nat = values[l, :, pl.ds(base, CH)]
                 do_masked = masked_pair(doT, e)
                 for copy in fetch(l, 2 * p + e, e):
                     copy.wait()
@@ -841,14 +902,16 @@
                 y1, y2 = farT[:HD], farT[HD:]
                 first_qf = first_q.astype(F32)
                 m = inv1 * jnp.sum(first_qf * y1, axis=0, keepdims=True)
-                cum = cum_ref[l, pl.ds(row, HD), :]
+                cum = cum_ref[pl.ds(row, HD), :]
                 dq = jnp.concatenate(near_q, axis=1)
                 dq = dq + (inv1 * (y1 - m * cum)) * slope1_q + (inv2 * y2) * (1.0 - second_q * second_q)
                 dpT_ref[pl.ds(row, HD), :] = dq.astype(BF16)
                 w_ref[pl.ds(row, HD), :] = (first_qf * (m * inv1)).astype(BF16)
-                for t0, t1 in WIDE:
+                after = 0.0
+                for t0, t1 in reversed(WIDE):
                     far = mm_nt(query_feat2[:CH, t0:], d_ref[t0:t1, t0:])
-                    back = mm_nt(w_ref[pl.ds(row, HD), t0:], wide_ref[t0:t1, t0:])
+                    back = mm_nt(w_ref[pl.ds(row, HD), t0:t1], wide_ref[:t1 - t0, :t1 - t0]) + after
+                    after = back[:, :1]
                     near_k = []
                     for u0 in range(t0, t1, CH):
                         u2 = min(u0 + 2 * CH, LEN)
@@ -892,7 +955,8 @@
     for l in reversed(range(LAYERS)):
         feed_backward(l)
         attention_backward(l)
-    dtable_sum = dtable_ref[...] + mm(placed(dx_ref[...].astype(BF16).T), hot)
+    dtable_head = sums_refs["grad_t"][:, :VOCAB].astype(F32) if linked else dtable_ref[...]
+    dtable_sum = dtable_head + mm(placed(dx_ref[...].astype(BF16).T), hot)
     if linked:
         sums_refs["grad_t"][:, :VOCAB] = dtable_sum.astype(BF16)
         sums_refs["grad_t"][:, VOCAB:] = placed(jnp.concatenate([dgains[...], jnp.zeros((120, D), F32)], axis=0).T).astype(BF16)
@@ -908,7 +972,7 @@
         dtable_ref[...] = dtable_sum
         for slot in range(4):
             pltpu.make_async_copy(stage.at[slot], dwo_ref.at[0], sem.at[slot]).wait()
-            pltpu.make_async_copy(stage_half.at[slot], dwe_ref.at[0, :, :BACK], sem_half.at[slot]).wait()
+            pltpu.make_async_copy(stage_half.at[slot], dwe_ref.at[0, :, :TILE], sem_half.at[slot]).wait()
 
 
 E0, E1, R0, R1, M0, M1, M2, M3, O, T = range(10)
@@ -916,118 +980,122 @@
 SHARED = ((False, False, True, False), (False, False, True, False))
 SERVICE = {
     (MIXER, 0): {
-        None: ((Links.second, 2), (Links.first, 3),),
+        None: ((Links.second, 2), (Links.first, 3), (Links.own, 5),),
     },
     (HEAD, 0): {
-        0: ((Links.own, 5),),
-        4: ((Links.first, 4),),
-        5: ((Links.second, 3),),
-        7: ((Links.own, 6),),
+        3: ((Links.first, 4),),
+        4: ((Links.second, 3),),
+        5: ((Links.own, 6),),
+        7: ((Links.own, 7),),
     },
     (OUTPUT, 0): {
         None: ((Links.ready, 2),),
     },
     (FEED, 0): {
-        None: ((Links.own, 7), (Links.third, 3), (Links.ready, 3),),
+        None: ((Links.first, 5), (Links.third, 3), (Links.ready, 3),),
     },
     (GELU, 0): {
         0: ((Links.second, 4), (Links.ready, 4),),
     },
     (FEED_TILE, 0): {
-        0: ((Links.first, 5), (Links.first, 6), (Links.own, 8),),
-        5: ((Links.first, 7),),
+        0: ((Links.first, 6), (Links.own, 8),),
+        1: ((Links.first, 7),),
+        3: ((Links.second, 5),),
     },
     (LAYER, 1): {
-        None: ((Links.second, 5), (Links.ready, 5),),
+        None: ((Links.ready, 5),),
     },
     (MIXER, 1): {
         None: ((Links.second, 6),),
     },
     (HEAD, 1): {
         1: ((Links.first, 8),),
-        3: ((Links.second, 7),),
-        7: ((Links.second, 8),),
+        2: ((Links.second, 7),),
+        6: ((Links.second, 8),),
+        7: ((Links.third, 7),),
     },
     (OUTPUT, 1): {
         None: ((Links.ready, 6),),
     },
     (FEED, 1): {
-        None: ((Links.third, 7), (Links.ready, 7),),
+        None: ((Links.ready, 7),),
     },
     (GELU, 1): {
         0: ((Links.ready, 8),),
     },
     (BACK_TILE, 1): {
-        3: ((E0, 1, 1),),
-        5: ((E0, 2, 1),),
+        1: ((E0, 1, 1), (Sums.tile_step, 0),),
+        2: ((Sums.tile_step, 1), (E0, 2, 1),),
+        3: ((Sums.tile_step, 2),),
     },
     (BACK_FEED, 1): {
         None: ((E1, 1, 1),),
     },
     (BACK_OUTPUT, 1): {
-        None: ((O, 1, 1), (R0, 2, 1), (R1, 2, 1),),
+        None: ((O, 1, 1),),
     },
     (BACK_HEAD, 1): {
-        0: ((E0, 3, 1), (E1, 2, 1), (O, 2, 1),),
-        2: ((R0, 3, 1), (M0, 2, 1),),
-        3: ((R1, 3, 1),),
-        4: ((E0, 4, 1), (M1, 2, 1),),
-        6: ((O, 3, 1), (M2, 2, 1),),
-        7: ((E0, 5, 1), (R0, 4, 1), (M0, 3, 1),),
+        0: ((E1, 2, 1), (R0, 2, 1), (R1, 2, 1), (O, 2, 1),),
+        1: ((E0, 3, 1),),
+        2: ((M0, 2, 1),),
+        3: ((E1, 3, 1),),
+        4: ((R0, 3, 1), (R1, 3, 1), (M1, 2, 1),),
+        5: ((E0, 4, 1), (O, 3, 1),),
+        6: ((M0, 3, 1), (M2, 2, 1), (E1, 4, 1),),
+        7: ((R0, 4, 1),),
     },
     (BACK_PAIR, 1): {
         0: ((M0, 1, 1),),
         1: ((M1, 1, 1),),
-        2: ((M2, 1, 1), (E1, 3, 1),),
+        2: ((M2, 1, 1),),
         3: ((M3, 1, 1),),
     },
     (BACK_MIXER, 1): {
-        None: ((R1, 4, 1), (M3, 2, 1),),
+        None: ((E0, 5, 1), (R1, 4, 1), (M3, 2, 1),),
     },
     (BACK_LAYER, 1): {
         None: ((M1, 3, 1),),
     },
     (BACK_TILE, 0): {
-        0: ((E0, 6, 1), (R0, 5, 1), (E1, 4, 1), (O, 4, 1), (M2, 3, 1),),
-        1: ((M0, 4, 1), (M3, 3, 1), (R1, 5, 1), (M1, 4, 1),),
-        2: ((M2, 4, 1),),
-        3: ((E0, 1, 0), (R0, 6, 1), (E1, 5, 1), (E0, 7, 1), (M3, 4, 1),),
-        4: ((O, 5, 1),),
-        5: ((R1, 6, 1), (M0, 5, 1), (M1, 5, 1), (E0, 2, 0),),
-        6: ((M2, 5, 1), (E1, 6, 1), (M3, 5, 1),),
-        7: ((O, 6, 1), (R0, 7, 1),),
+        0: ((E1, 5, 1), (M0, 4, 1), (O, 4, 1), (M2, 3, 1), (M1, 4, 1), (M3, 3, 1),),
+        1: ((E0, 1, 0), (Sums.tile_step, 0), (E0, 6, 1), (R0, 5, 1),),
+        2: ((Sums.tile_step, 1), (E1, 6, 1), (R1, 5, 1), (M0, 5, 1), (M2, 4, 1), (M3, 4, 1), (E0, 2, 0),),
+        3: ((Sums.tile_step, 2), (R0, 6, 1), (M1, 5, 1), (O, 5, 1),),
     },
     (BACK_FEED, 0): {
         None: ((E1, 1, 0),),
     },
     (BACK_OUTPUT, 0): {
-        None: ((O, 1, 0), (M0, 6, 1), (R0, 2, 0), (M1, 6, 1),),
+        None: ((O, 1, 0), (M2, 5, 1), (M3, 5, 1), (E0, 7, 1),),
     },
     (BACK_HEAD, 0): {
-        0: ((M2, 6, 1), (M3, 6, 1), (R1, 7, 1), (E0, 3, 0), (R1, 2, 0),),
-        1: ((E1, 7, 1), (E1, 2, 0),),
-        2: ((M0, 7, 1), (O, 7, 1), (R0, 3, 0), (E0, 4, 0), (M0, 2, 0), (O, 2, 0),),
-        3: ((M1, 7, 1), (M2, 7, 1),),
-        4: ((M3, 7, 1), (R1, 3, 0), (E0, 5, 0), (M1, 2, 0),),
-        5: ((E1, 3, 0),),
-        6: ((R0, 4, 0), (M2, 2, 0), (M0, 3, 0),),
-        7: ((E0, 6, 0), (O, 3, 0),),
+        0: ((R1, 6, 1), (E1, 7, 1), (E1, 2, 0), (M0, 6, 1), (R0, 2, 0), (R1, 2, 0), (O, 2, 0),),
+        1: ((M1, 6, 1), (E0, 3, 0),),
+        2: ((M2, 6, 1), (R0, 7, 1), (M0, 2, 0),),
+        3: ((M3, 6, 1), (E1, 3, 0),),
+        4: ((R1, 7, 1), (M0, 7, 1), (R0, 3, 0), (R1, 3, 0), (M1, 2, 0),),
+        5: ((M1, 7, 1), (E0, 4, 0), (O, 7, 1), (O, 3, 0),),
+        6: ((M2, 7, 1), (M3, 7, 1), (M0, 3, 0), (E1, 4, 0), (M2, 2, 0),),
+        7: ((E0, 5, 0), (R0, 4, 0),),
     },
     (BACK_PAIR, 0): {
-        0: ((M0, 1, 0),),
+        0: ((M0, 1, 0), (O, 6, 1),),
         1: ((M1, 1, 0),),
         2: ((M2, 1, 0),),
         3: ((M3, 1, 0),),
     },
     (BACK_MIXER, 0): {
-        None: ((R0, 5, 0), (R1, 4, 0), (M3, 2, 0), (M1, 3, 0),),
+        None: ((R1, 4, 0), (M3, 2, 0),),
+    },
+    (BACK_LAYER, 0): {
+        None: ((E1, 5, 0), (M1, 3, 0), (O, 4, 0),),
     },
     (END, 0): {
         None: (
-            (T, 1, 0), (E1, 4, 0), (M2, 3, 0), (T, 2, 0), (M0, 4, 0), (R1, 5, 0), (O, 4, 0), (M3, 3, 0), (R0, 6, 0), (M1, 4, 0),
-            (M2, 4, 0), (E1, 5, 0), (T, 3, 0), (M0, 5, 0), (M3, 4, 0), (O, 5, 0), (R1, 6, 0), (T, 4, 0), (M1, 5, 0), (M2, 5, 0),
-            (E1, 6, 0), (M3, 5, 0), (M0, 6, 0), (T, 5, 0), (O, 6, 0), (M1, 6, 0), (M2, 6, 0), (M3, 6, 0), (T, 6, 0), (E0, 7, 0),
-            (R0, 7, 0), (R1, 7, 0), (E1, 7, 0), (M0, 7, 0), (O, 7, 0), (M1, 7, 0), (M2, 7, 0), (M3, 7, 0), (T, 7, 0),
+            (T, 1, 0), (M0, 4, 0), (M2, 3, 0), (T, 2, 0), (E0, 6, 0), (M3, 3, 0), (R0, 5, 0), (M1, 4, 0), (M2, 4, 0),
+            (E1, 6, 0), (R1, 5, 0), (T, 3, 0), (M3, 4, 0), (O, 5, 0), (M0, 5, 0), (R0, 6, 0), (T, 4, 0), (M1, 5, 0), (M2, 5, 0),
+            (R1, 6, 0), (M3, 5, 0), (T, 5, 0), (O, 6, 0), (M0, 6, 0), (M1, 6, 0), (M2, 6, 0), (M3, 6, 0), (T, 6, 0), (E0, 7, 0),
+            (E1, 7, 0), (R0, 7, 0), (R1, 7, 0), (O, 7, 0), (M0, 7, 0), (M1, 7, 0), (M2, 7, 0), (M3, 7, 0), (T, 7, 0),
         ),
     },
 }
@@ -1040,15 +1108,16 @@
     x=pltpu.VMEM((LAYERS, LEN, D), F32),
     x1=pltpu.VMEM((LAYERS, LEN, D), F32),
     dx=pltpu.VMEM((LEN, D), F32),
-    kv=pltpu.VMEM((LAYERS, LEN, 2 * D), BF16),
+    keys=pltpu.VMEM((LEN, D), BF16),
+    values=pltpu.VMEM((LAYERS, LEN, D), BF16),
     pT=pltpu.VMEM((LAYERS, 3 * D, LEN), BF16),
     inv1s=pltpu.VMEM((LAYERS, HEADS, 1, LEN), F32),
-    cum=pltpu.VMEM((LAYERS, D, LEN), F32),
+    cum=pltpu.VMEM((D, LEN), F32),
     oT=pltpu.VMEM((LAYERS, D, LEN), BF16),
     hT=pltpu.VMEM((LAYERS, D, LEN), BF16),
     g=pltpu.VMEM((LEN, D), BF16),
     gT=pltpu.VMEM((LAYERS, D, LEN), BF16),
-    wide=pltpu.VMEM((LEN, LEN), BF16),
+    wide=pltpu.VMEM((2 * CH, 2 * CH), BF16),
     a1k=pltpu.VMEM((D, LEN), BF16),
     m=pltpu.VMEM((2, LEN, LEN), BF16),
     near=pltpu.VMEM((2, CHUNKS, CH + REACH, CH), F32),
@@ -1062,7 +1131,7 @@
 )
 PLAIN_SCRATCH = dict(
     stage=pltpu.VMEM((4, D, TILE), BF16),
-    stage_half=pltpu.VMEM((4, D, BACK), BF16),
+    stage_half=pltpu.VMEM((4, D, TILE), BF16),
     sem=pltpu.SemaphoreType.DMA((4,)),
     sem_half=pltpu.SemaphoreType.DMA((4,)),
 )
@@ -1076,7 +1145,7 @@
         "grad_" + n: pltpu.VMEM((rows, cols), BF16),
         "r1" + n: pltpu.VMEM(shape(4), BF16),
         "r2" + n: pltpu.VMEM(shape(2), BF16),
-        "r3" + n: pltpu.VMEM(shape(1), BF16),
+        "r3" + n: pltpu.VMEM((1 if n == "t" else LAYERS,) + shape(1), BF16),
         "rz" + n: pltpu.VMEM((2,) + shape(1), BF16),
     }
 
@@ -1097,11 +1166,10 @@
     zsend=pltpu.SemaphoreType.DMA((3, 4)),
     zrecv=pltpu.SemaphoreType.DMA((3, 4)),
     load_sem=pltpu.SemaphoreType.DMA((LAYERS, 9)),
-    sum_send=pltpu.SemaphoreType.DMA((10, 10)),
-    sum_recv=pltpu.SemaphoreType.DMA((10, 9)),
+    sum_send=pltpu.SemaphoreType.DMA((10, 11)),
+    sum_recv=pltpu.SemaphoreType.DMA((10, 11)),
     tile_send=pltpu.SemaphoreType.DMA((4,)),
     tile_recv=pltpu.SemaphoreType.DMA((4,)),
-    dtable=pltpu.VMEM((D, VOCAB), F32),
     dgains=pltpu.VMEM((8, D), F32),
     **sum_buffers("m", D, 3 * D, 0),
     **sum_buffers("o", D, D, 0),

time: 190 us -> 170 us (0.89); the launches traced: 190 us -> 168 us
  Pallas kernels: 188 us -> 165 us
    pallas_call x1, Pallas kernels: 184 us -> 162 us  [local_step(): pl.pallas_call(functools.partial(step_kernel, linked), out_shape=out_shap...]
where the time goes in v1:
time: 170 us; the launch traced here: 168 us
  Pallas kernels  165 us (97%)
    pallas_call x1, Pallas kernels, local_step(): pl.pallas_call(functools.partial(step_kernel, linked), out_shape=out_shap...  162 us
    pallas_call x1, Pallas kernels, finish(): pl.pallas_call(finish_kernel, out_shape=tuple((jax.ShapeDtypeStruct(shape...  3.68 us

profile of v1, /device:TPU:0, one launch (start us, length us, event | category | flops | bytes accessed | tf_op | source)
XLA Modules:
  0.0 167.6 jit_solution(12559655816347179518)
XLA Ops:
  0.6 161.7 %local_step.1 = (f32[4,8,128]{2,1,0:T(8,128)}, bf16[4,64,640]{2,1,0:T(8,128)(2,1)}, bf16[2,8,640,640]{3,2,1,0:T(8,128)(2,1)}, f32[2,8,5,160,128]{4,3,2,1,0:T(8,1...) custom-call(s32[4,640]{1,0:T(4,128)} %refs_0_.1, ...), custom_call_target="tpu_custom_call" | custom-call | flops 40000000000 | bytes 40000000 | tf_op jit(solution)/shard_map/local_step/pallas_call | solution.py:1218
  162.3 3.7 %finish.1 = (f32[1,128]{1,0:T(1,128)}, f32[4,64,640]{2,1,0:T(8,128)}, f32[64,64]{1,0:T(8,128)}, f32[2,64,1536]{2,1,0:T(8,128)}, f32[2,64,512]{2,1,0:T(8,128)}, /...) custom-call(f32[4,8,128]{2,1,0:T(8,128)} %get-tuple-element.27.loss_, ...), custom_call_target="tpu_custom_call" | custom-call | tf_op jit(solution)/shard_map/finish/pallas_call | solution.py:1269
  166.0 1.1 slice_bitcast_fusion

commit v2 on v1

--- a/solution.py
+++ b/solution.py
@@ -536,7 +536,6 @@
             pl.semaphore_signal(barrier, inc=1, device_id={DP: target}, device_id_type=pl.DeviceIdType.MESH)
         for k in (1, 2, 3):
             pl.semaphore_signal(barrier, inc=1, device_id={SECTION: (zi + k) % 4}, device_id_type=pl.DeviceIdType.MESH)
-        pl.semaphore_wait(barrier, 6)
 
         own64 = pl.ds(pl.multiple_of(links.d * 64, 64), 64)
         own256 = pl.ds(pl.multiple_of(links.d * 256, 256), 256)
@@ -547,9 +546,10 @@
         gathered = jnp.concatenate([gathered, jnp.zeros((120, 128), F32)], axis=0).T[:64]
         small_b = (jnp.concatenate([emb[...], jnp.zeros((64, 64), F32)], axis=1) + pltpu.roll(gathered, 64, 1)).astype(BF16)
         tz[zi] = small_b
+        take(0, "m")
+        pl.semaphore_wait(barrier, 6)
         for k in (1, 2, 3):
             table_copy(k).start()
-        take(0, "m")
         links.own(1)
         r, c = iotas(8, LEN)
         ids = tokens[pl.ds(zi, 1), :].astype(F32)
@@ -977,42 +977,42 @@
 
 E0, E1, R0, R1, M0, M1, M2, M3, O, T = range(10)
 MIXER, HEAD, FEED, GELU, FEED_TILE, LAYER, BACK_TILE, BACK_FEED, BACK_OUTPUT, BACK_HEAD, BACK_PAIR, BACK_MIXER, BACK_LAYER, END, OUTPUT = range(15)
-SHARED = ((False, False, True, False), (False, False, True, False))
+SHARED = ((False, False, True, False), (True, False, True, False))
 SERVICE = {
     (MIXER, 0): {
-        None: ((Links.second, 2), (Links.first, 3), (Links.own, 5),),
+        None: ((Links.second, 2), (Links.first, 3),),
     },
     (HEAD, 0): {
+        1: ((Links.own, 5),),
         3: ((Links.first, 4),),
         4: ((Links.second, 3),),
         5: ((Links.own, 6),),
+        6: ((Links.first, 5),),
         7: ((Links.own, 7),),
     },
     (OUTPUT, 0): {
         None: ((Links.ready, 2),),
     },
     (FEED, 0): {
-        None: ((Links.first, 5), (Links.third, 3), (Links.ready, 3),),
+        None: ((Links.second, 4), (Links.third, 3), (Links.ready, 3),),
     },
     (GELU, 0): {
-        0: ((Links.second, 4), (Links.ready, 4),),
+        0: ((Links.ready, 4),),
     },
     (FEED_TILE, 0): {
-        0: ((Links.first, 6), (Links.own, 8),),
-        1: ((Links.first, 7),),
-        3: ((Links.second, 5),),
+        0: ((Links.second, 5), (Links.first, 6), (Links.own, 8),),
+        2: ((Links.first, 7),),
     },
     (LAYER, 1): {
-        None: ((Links.ready, 5),),
+        None: ((Links.third, 5), (Links.ready, 5),),
     },
     (MIXER, 1): {
-        None: ((Links.second, 6),),
+        None: ((Links.second, 6), (Links.first, 8),),
     },
     (HEAD, 1): {
-        1: ((Links.first, 8),),
-        2: ((Links.second, 7),),
-        6: ((Links.second, 8),),
-        7: ((Links.third, 7),),
+        0: ((Links.second, 7),),
+        4: ((Links.second, 8),),
+        5: ((Links.third, 7),),
     },
     (OUTPUT, 1): {
         None: ((Links.ready, 6),),
@@ -1025,81 +1025,79 @@
     },
     (BACK_TILE, 1): {
         1: ((E0, 1, 1), (Sums.tile_step, 0),),
-        2: ((Sums.tile_step, 1), (E0, 2, 1),),
+        2: ((Sums.tile_step, 1),),
         3: ((Sums.tile_step, 2),),
     },
     (BACK_FEED, 1): {
         None: ((E1, 1, 1),),
     },
     (BACK_OUTPUT, 1): {
-        None: ((O, 1, 1),),
+        None: ((O, 1, 1), (E0, 2, 1),),
     },
     (BACK_HEAD, 1): {
-        0: ((E1, 2, 1), (R0, 2, 1), (R1, 2, 1), (O, 2, 1),),
-        1: ((E0, 3, 1),),
-        2: ((M0, 2, 1),),
-        3: ((E1, 3, 1),),
-        4: ((R0, 3, 1), (R1, 3, 1), (M1, 2, 1),),
-        5: ((E0, 4, 1), (O, 3, 1),),
-        6: ((M0, 3, 1), (M2, 2, 1), (E1, 4, 1),),
-        7: ((R0, 4, 1),),
+        0: ((E1, 2, 1), (R0, 2, 1),),
+        2: ((E0, 3, 1),),
+        3: ((R1, 2, 1), (M0, 2, 1),),
+        4: ((E1, 3, 1), (R0, 3, 1), (R1, 3, 1),),
+        5: ((E0, 4, 1),),
+        6: ((E1, 4, 1), (M1, 2, 1),),
+        7: ((R0, 4, 1), (M2, 2, 1),),
     },
     (BACK_PAIR, 1): {
         0: ((M0, 1, 1),),
         1: ((M1, 1, 1),),
-        2: ((M2, 1, 1),),
-        3: ((M3, 1, 1),),
+        2: ((M2, 1, 1), (M0, 3, 1),),
+        3: ((M3, 1, 1), (O, 2, 1),),
     },
     (BACK_MIXER, 1): {
-        None: ((E0, 5, 1), (R1, 4, 1), (M3, 2, 1),),
+        None: ((E0, 5, 1), (R1, 4, 1), (M0, 4, 1), (M3, 2, 1),),
     },
     (BACK_LAYER, 1): {
         None: ((M1, 3, 1),),
     },
     (BACK_TILE, 0): {
-        0: ((E1, 5, 1), (M0, 4, 1), (O, 4, 1), (M2, 3, 1), (M1, 4, 1), (M3, 3, 1),),
-        1: ((E0, 1, 0), (Sums.tile_step, 0), (E0, 6, 1), (R0, 5, 1),),
-        2: ((Sums.tile_step, 1), (E1, 6, 1), (R1, 5, 1), (M0, 5, 1), (M2, 4, 1), (M3, 4, 1), (E0, 2, 0),),
-        3: ((Sums.tile_step, 2), (R0, 6, 1), (M1, 5, 1), (O, 5, 1),),
+        0: ((E1, 5, 1), (M2, 3, 1), (M3, 3, 1), (O, 3, 1),),
+        1: ((E0, 1, 0), (Sums.tile_step, 0), (E0, 6, 1), (R0, 5, 1), (M1, 4, 1),),
+        2: ((Sums.tile_step, 1), (E1, 6, 1), (R1, 5, 1), (M0, 5, 1), (M2, 4, 1), (M3, 4, 1), (O, 4, 1), (E0, 2, 0),),
+        3: ((Sums.tile_step, 2), (R0, 6, 1), (M1, 5, 1), (M2, 5, 1), (E0, 7, 1),),
     },
     (BACK_FEED, 0): {
         None: ((E1, 1, 0),),
     },
     (BACK_OUTPUT, 0): {
-        None: ((O, 1, 0), (M2, 5, 1), (M3, 5, 1), (E0, 7, 1),),
+        None: ((O, 1, 0), (M3, 5, 1), (R0, 2, 0),),
     },
     (BACK_HEAD, 0): {
-        0: ((R1, 6, 1), (E1, 7, 1), (E1, 2, 0), (M0, 6, 1), (R0, 2, 0), (R1, 2, 0), (O, 2, 0),),
-        1: ((M1, 6, 1), (E0, 3, 0),),
-        2: ((M2, 6, 1), (R0, 7, 1), (M0, 2, 0),),
-        3: ((M3, 6, 1), (E1, 3, 0),),
-        4: ((R1, 7, 1), (M0, 7, 1), (R0, 3, 0), (R1, 3, 0), (M1, 2, 0),),
-        5: ((M1, 7, 1), (E0, 4, 0), (O, 7, 1), (O, 3, 0),),
-        6: ((M2, 7, 1), (M3, 7, 1), (M0, 3, 0), (E1, 4, 0), (M2, 2, 0),),
-        7: ((E0, 5, 0), (R0, 4, 0),),
+        0: ((R1, 6, 1), (M0, 6, 1), (O, 5, 1), (E1, 7, 1), (E1, 2, 0), (E0, 3, 0),),
+        1: ((M1, 6, 1), (M2, 6, 1), (M3, 6, 1), (R0, 7, 1), (R0, 3, 0),),
+        2: ((O, 6, 1), (R1, 2, 0), (R1, 3, 0),),
+        3: ((R1, 7, 1), (E1, 3, 0),),
+        4: ((M1, 7, 1), (M2, 7, 1), (R0, 4, 0), (M0, 2, 0),),
+        5: ((M3, 7, 1), (R1, 4, 0), (M1, 2, 0),),
+        6: ((M0, 3, 0), (M2, 2, 0),),
+        7: ((R0, 5, 0), (M1, 3, 0),),
     },
     (BACK_PAIR, 0): {
-        0: ((M0, 1, 0), (O, 6, 1),),
-        1: ((M1, 1, 0),),
-        2: ((M2, 1, 0),),
+        0: ((M0, 1, 0),),
+        1: ((M1, 1, 0), (M0, 7, 1), (E0, 4, 0),),
+        2: ((M2, 1, 0), (O, 7, 1), (E0, 5, 0), (E1, 4, 0), (O, 2, 0),),
         3: ((M3, 1, 0),),
     },
     (BACK_MIXER, 0): {
-        None: ((R1, 4, 0), (M3, 2, 0),),
+        None: ((E0, 6, 0), (R1, 5, 0), (M0, 4, 0), (O, 3, 0), (M3, 2, 0),),
     },
     (BACK_LAYER, 0): {
-        None: ((E1, 5, 0), (M1, 3, 0), (O, 4, 0),),
+        None: ((M1, 4, 0), (M2, 3, 0),),
     },
     (END, 0): {
         None: (
-            (T, 1, 0), (M0, 4, 0), (M2, 3, 0), (T, 2, 0), (E0, 6, 0), (M3, 3, 0), (R0, 5, 0), (M1, 4, 0), (M2, 4, 0),
-            (E1, 6, 0), (R1, 5, 0), (T, 3, 0), (M3, 4, 0), (O, 5, 0), (M0, 5, 0), (R0, 6, 0), (T, 4, 0), (M1, 5, 0), (M2, 5, 0),
-            (R1, 6, 0), (M3, 5, 0), (T, 5, 0), (O, 6, 0), (M0, 6, 0), (M1, 6, 0), (M2, 6, 0), (M3, 6, 0), (T, 6, 0), (E0, 7, 0),
-            (E1, 7, 0), (R0, 7, 0), (R1, 7, 0), (O, 7, 0), (M0, 7, 0), (M1, 7, 0), (M2, 7, 0), (M3, 7, 0), (T, 7, 0),
+            (T, 1, 0), (E1, 5, 0), (T, 2, 0), (R0, 6, 0), (O, 4, 0), (M0, 5, 0), (M3, 3, 0), (M1, 5, 0), (M2, 4, 0), (R1, 6, 0),
+            (O, 5, 0), (T, 3, 0), (M2, 5, 0), (M3, 4, 0), (E1, 6, 0), (M3, 5, 0), (M0, 6, 0), (T, 4, 0), (M1, 6, 0), (T, 5, 0),
+            (O, 6, 0), (M2, 6, 0), (M3, 6, 0), (T, 6, 0), (E0, 7, 0), (R0, 7, 0), (R1, 7, 0), (E1, 7, 0), (M0, 7, 0),
+            (M1, 7, 0), (O, 7, 0), (M2, 7, 0), (M3, 7, 0), (T, 7, 0),
         ),
     },
 }
-
 PLAIN_IN = ("columns", "table", "gm", "gf", "gz", "wm", "wo", "we", "wr")
 PLAIN_OUT = ("loss", "lg", "kept_m", "kept_near", "dtable", "dgm", "dgf", "dgz", "dwm", "dwo", "dwe", "dwrt")
 LINKED_IN = ("tokens", "mask", "emb", "mgain", "fgain", "zgain", "wm_s", "wo_s", "we_s", "wr_s")
@@ -1231,48 +1229,67 @@
     )(*operands)
 
 
-def finish_kernel(
-    loss_in, lg_in, dwm_in, dwo_in, dwe_in, dwrt_in, last_in,
-    out_loss, out_lg, out_table, out_m, out_o, out_mgain, out_e, out_r, out_fgain, out_zgain,
-    loss, lg, dwm, dwo, dwe, dwrt, last, sem,
-):
-    pairs = ((loss_in, loss), (lg_in, lg), (dwm_in, dwm), (dwo_in, dwo), (dwe_in, dwe), (dwrt_in, dwrt), (last_in, last))
-    copies = [pltpu.make_async_copy(src, dst, sem.at[i]) for i, (src, dst) in enumerate(pairs)]
+def finish_kernel(*refs):
+    count = 7
+    ins, outs = refs[:count], refs[count:count + 10]
+    held, made = refs[count + 10:2 * count + 10], refs[2 * count + 10:2 * count + 20]
+    in_sem, out_sem = refs[2 * count + 20:]
+    copies = [pltpu.make_async_copy(src, dst, in_sem.at[i]) for i, (src, dst) in enumerate(zip(ins, held))]
+    leave = [pltpu.make_async_copy(src, dst, out_sem.at[i]) for i, (src, dst) in enumerate(zip(made, outs))]
     every(copies, START)
-    every(copies, WAIT)
+    loss, lg, dwm, dwo, dwe, dwrt, last = held
+    out_loss, out_lg, out_table, out_m, out_o, out_mgain, out_e, out_r, out_fgain, out_zgain = made
     z = lax.axis_index(SECTION)
-    r, c = iotas(4, 128)
-    out_loss[...] = jnp.sum(jnp.where(r == c, loss[:, 0, :], 0.0), axis=0, keepdims=True)
+    copies[4].wait()
+    out_e[...] = dwe[...].astype(F32)
+    leave[6].start()
+    copies[1].wait()
     out_lg[...] = lg[...].astype(F32)
+    leave[1].start()
+    copies[2].wait()
+    for l in range(LAYERS):
+        for p in range(4):
+            for j in range(3):
+                out_m[l, :, D * j + CH * p:D * j + CH * (p + 1)] = dwm[l, p, :, CH * j:CH * (j + 1)].astype(F32)
+    leave[3].start()
+    copies[5].wait()
+    for l in range(LAYERS):
+        out_r[l] = dwrt[l].astype(F32).T
+    leave[7].start()
+    copies[3].wait()
+    out_o[...] = dwo[...].astype(F32)
+    leave[4].start()
+    copies[6].wait()
     table = last[:, :VOCAB].astype(F32)
     out_table[...] = sum(jnp.where(z == i, table[:, 64 * i:64 * (i + 1)], 0.0) for i in range(4))
+    leave[2].start()
     gains = last[:, VOCAB:].astype(F32)
     gains = jnp.concatenate([gains, jnp.zeros((64, 128), F32)], axis=0).T
     out_mgain[...] = gains[0:2, :64]
     out_fgain[...] = gains[2:4, :64]
     out_zgain[...] = gains[4:5, :64]
-    out_o[...] = dwo[...].astype(F32)
-    out_e[...] = dwe[...].astype(F32)
-    for l in range(LAYERS):
-        out_r[l] = dwrt[l].astype(F32).T
-        for p in range(4):
-            for j in range(3):
-                out_m[l, :, D * j + CH * p:D * j + CH * (p + 1)] = dwm[l, p, :, CH * j:CH * (j + 1)].astype(F32)
+    copies[0].wait()
+    r, c = iotas(4, 128)
+    out_loss[...] = jnp.sum(jnp.where(r == c, loss[:, 0, :], 0.0), axis=0)[:4]
+    for i in (5, 8, 9, 0):
+        leave[i].start()
+    every(leave, WAIT)
 
 
 def finish(*operands):
-    vmem = pl.BlockSpec(memory_space=pltpu.VMEM)
+    hbm = pl.BlockSpec(memory_space=pl.ANY)
     shapes = (
-        (1, 128), (4, 64, LEN), (64, 64), (LAYERS, 64, 3 * D), (LAYERS, 64, D), (LAYERS, 64), (LAYERS, 64, FF),
+        (4,), (4, 64, LEN), (64, 64), (LAYERS, 64, 3 * D), (LAYERS, 64, D), (LAYERS, 64), (LAYERS, 64, FF),
         (LAYERS, 256, D), (LAYERS, 64), (1, 64),
     )
     return pl.pallas_call(
         finish_kernel,
         out_shape=tuple(jax.ShapeDtypeStruct(shape, F32) for shape in shapes),
-        in_specs=[pl.BlockSpec(memory_space=pl.ANY)] * len(operands),
-        out_specs=(vmem,) * len(shapes),
+        in_specs=[hbm] * len(operands),
+        out_specs=(hbm,) * len(shapes),
         scratch_shapes=[pltpu.VMEM(operand.shape, operand.dtype) for operand in operands]
-        + [pltpu.SemaphoreType.DMA((len(operands),))],
+        + [pltpu.VMEM(shape, F32) for shape in shapes]
+        + [pltpu.SemaphoreType.DMA((len(operands),)), pltpu.SemaphoreType.DMA((len(shapes),))],
         compiler_params=pltpu.CompilerParams(vmem_limit_bytes=60 * 1024 * 1024),
         name="finish",
     )(*operands)
@@ -1305,7 +1322,7 @@
             loss, lg, dwm, dwo, dwe, dwrt, last
         )
         return (
-            loss[0, :4], jnp.swapaxes(lg, 1, 2), table_grad, dwm, dwo, mixer_gain_grad, dwe, dwr, feed_gain_grad, final_gain_grad[0]
+            loss, jnp.swapaxes(lg, 1, 2), table_grad, dwm, dwo, mixer_gain_grad, dwe, dwr, feed_gain_grad, final_gain_grad[0]
         )
 
     token_row = lax.dynamic_index_in_dim(tokens, segment_index, 0, keepdims=False)

time: 170 us -> 166 us (0.976)
  Pallas kernels: 165 us -> 162 us
    pallas_call x1, Pallas kernels: 162 us -> 159 us  [local_step(): pl.pallas_call(functools.partial(step_kernel, linked), out_shape=out_shap...]
where the time goes in v2:
time: 166 us; the launch traced here: 163 us
  Pallas kernels  162 us (98%)
    pallas_call x1, Pallas kernels, local_step(): pl.pallas_call(functools.partial(step_kernel, linked), out_shape=out_shap...  159 us
    pallas_call x1, Pallas kernels, finish(): pl.pallas_call(finish_kernel, out_shape=tuple((jax.ShapeDtypeStruct(shape...  3.42 us

profile of v2, /device:TPU:0, one launch (start us, length us, event | category | flops | bytes accessed | tf_op | source)
XLA Modules:
  0.0 163.2 jit_solution(3714067982202817517)
XLA Ops:
  0.6 158.7 %local_step.1 = (f32[4,8,128]{2,1,0:T(8,128)}, bf16[4,64,640]{2,1,0:T(8,128)(2,1)}, bf16[2,8,640,640]{3,2,1,0:T(8,128)(2,1)}, f32[2,8,5,160,128]{4,3,2,1,0:T(8,1...) custom-call(s32[4,640]{1,0:T(4,128)} %refs_0_.1, ...), custom_call_target="tpu_custom_call" | custom-call | flops 40000000000 | bytes 40000000 | tf_op jit(solution)/shard_map/local_step/pallas_call | solution.py:1216
  159.3 3.4 %finish.1 = (f32[4]{0:T(128)}, f32[4,64,640]{2,1,0:T(8,128)}, f32[64,64]{1,0:T(8,128)}, f32[2,64,1536]{2,1,0:T(8,128)}, f32[2,64,512]{2,1,0:T(8,128)}, /*index=5...) custom-call(f32[4,8,128]{2,1,0:T(8,128)} %get-tuple-element.27.refs_0_, ...), custom_call_target="tpu_custom_call" | custom-call | tf_op jit(solution)/shard_map/finish/pallas_call | solution.py:1285

commit v3 on v2

--- a/solution.py
+++ b/solution.py
@@ -710,8 +710,8 @@
                 total = jnp.sum(first_q * cum_ref[pl.ds(row, HD), :], axis=0, keepdims=True)
                 inv1 = 1.0 / (total + 1.0)
                 inv1_ref[l, 2 * p + e] = inv1
-                query_feat2 = query_features(qT, inv1, inv2)[3]
-                key_feat2 = jnp.concatenate([key_feat, key_feat], axis=1)
+                query_feat2 = query_features(qT, inv1, inv2)[3][:CH]
+                key_feat2 = key_feat
                 key_nat = keys[:, pl.ds(base, CH)]
                 query_masked = masked_pair(qT, e)
                 for t0, t1 in WIDE:

time: 166 us -> 165 us (level)
  no operation moved by 1% of the time
where the time goes in v3:
time: 165 us; the launch traced here: 162 us
  Pallas kernels  161 us (98%)
    pallas_call x1, Pallas kernels, local_step(): pl.pallas_call(functools.partial(step_kernel, linked), out_shape=out_shap...  158 us
    pallas_call x1, Pallas kernels, finish(): pl.pallas_call(finish_kernel, out_shape=tuple((jax.ShapeDtypeStruct(shape...  3.42 us

profile of v3, /device:TPU:0, one launch (start us, length us, event | category | flops | bytes accessed | tf_op | source)
XLA Modules:
  0.0 162.2 jit_solution(3129549327528941405)
XLA Ops:
  0.6 157.6 %local_step.1 = (f32[4,8,128]{2,1,0:T(8,128)}, bf16[4,64,640]{2,1,0:T(8,128)(2,1)}, bf16[2,8,640,640]{3,2,1,0:T(8,128)(2,1)}, f32[2,8,5,160,128]{4,3,2,1,0:T(8,1...) custom-call(s32[4,640]{1,0:T(4,128)} %refs_0_.1, ...), custom_call_target="tpu_custom_call" | custom-call | flops 40000000000 | bytes 40000000 | tf_op jit(solution)/shard_map/local_step/pallas_call | solution.py:1216
  158.3 3.4 %finish.1 = (f32[4]{0:T(128)}, f32[4,64,640]{2,1,0:T(8,128)}, f32[64,64]{1,0:T(8,128)}, f32[2,64,1536]{2,1,0:T(8,128)}, f32[2,64,512]{2,1,0:T(8,128)}, /*index=5...) custom-call(f32[4,8,128]{2,1,0:T(8,128)} %get-tuple-element.27.refs_0_, ...), custom_call_target="tpu_custom_call" | custom-call | tf_op jit(solution)/shard_map/finish/pallas_call | solution.py:1285
